TPU v7x, 32 devices: a whole 2x2x4 slice. The times are simulated.
32 devices in a mesh: dp: 4 (over x, core), ep: 2 (over y), cp: 4 (over z).
Axes of the slice: x: 2, y: 2, z: 4, core: 2. Of those that a mesh axis runs over, the one named last changes fastest.
Arguments:
- tokens: bfloat16 [1024, 16, 1024], P('cp', ('dp', 'ep')), may hold values from -6 to 6
- lengths: int32 [16], P(('dp', 'ep')), may hold values from 256 to 1024, as said below
- expert_ids: int32 [1024, 16, 2], P('cp', ('dp', 'ep')), may hold values from 0 to 3, as said below
- places: int32 [1024, 16, 2], P('cp', ('dp', 'ep')), may hold values from -1 to 319, as said below
- buckets: int32 [1024], replicated, may hold values from 0 to 31, as said below
- w_attn: bfloat16 [1024, 4096], replicated
- bias_table: float32 [16, 32], replicated, may hold values from -4 to 4
- norm1_gain: float32 [1024], replicated, may hold values from 0.5 to 1.5
- norm2_gain: float32 [1024], replicated, may hold values from 0.5 to 1.5
- w_router: bfloat16 [1024, 4], replicated, may hold values from -0.125 to 0.125
- w_gate: bfloat16 [4, 1024, 2816], P('ep'), may hold values from -0.1875 to 0.1875
- w_up: bfloat16 [4, 1024, 2816], P('ep'), may hold values from -0.1875 to 0.1875
- w_down: bfloat16 [4, 1024, 2816], P('ep'), may hold values from -1.25 to 1.25
- cotangent: bfloat16 [1024, 16, 1024], P('cp', ('dp', 'ep')), may hold values from -6 to 6
Outputs:
- mixed: bfloat16 [1024, 16, 1024], P('cp', ('dp', 'ep'))
- tokens_grad: bfloat16 [1024, 16, 1024], P('cp', ('dp', 'ep'))
- w_attn_grad: float32 [1024, 4096], P(None, ('dp', 'ep', 'cp'))
- bias_table_grad: float32 [16, 32], replicated
- norm1_gain_grad: float32 [1024], replicated
- norm2_gain_grad: float32 [1024], replicated
- w_router_grad: float32 [1024, 4], replicated
- w_gate_grad: float32 [4, 1024, 2816], P('ep', None, ('dp', 'cp'))
- w_up_grad: float32 [4, 1024, 2816], P('ep', None, ('dp', 'cp'))
- w_down_grad: float32 [4, 1024, 2816], P('ep', None, ('dp', 'cp'))
Inputs may be any that keep to these rules, and one draw needn't show every extreme that they name: `lengths`: in each group of 2 slots held by one index of dp+ep, one slot has length 1024. `expert_ids`: the 2 experts of a token differ. -1 for padding positions and for choices beyond an expert's places; within the rows of one device the routed choices of one expert have distinct places. `buckets`: Non-decreasing in the distance, 0 at distance 0.
All inputs are finite; a program needn't handle non-finite values.
Results may differ from a plain program's by a relative error of at most 0.02.
Values may be sent and summed in bfloat16 or wider, within the bound.
A program may use at most 320 MiB of HBM per device.

v0:
```python
import functools

import jax
import jax.numpy as jnp
from jax import lax
from jax.experimental import pallas as pl
from jax.experimental.pallas import tpu as pltpu
from jax.sharding import PartitionSpec as P

epsilon = 1e-06
masked_value = -1000000000.0


def gelu_tanh(values):
    return jax.nn.gelu(values, approximate=True)


def root_scale(values):
    return lax.rsqrt(jnp.mean(values * values, axis=-1, keepdims=True) + epsilon)


def norm_back(grad_in, values, scale_rows, gain_vector):
    scaled = grad_in * gain_vector
    inner_mean = jnp.mean(scaled * values, axis=-1, keepdims=True)
    return scale_rows * (scaled - values * scale_rows * scale_rows * inner_mean)


def block_logits(
    queries, key_rows, key_start, query_pos, lengths, table_step, rise_points, head_scale
):
    key_count = key_rows.shape[0]
    key_pos = key_start + jnp.arange(key_count, dtype=jnp.int32)
    scores = (
        jnp.einsum("qshd,kshd->shqk", queries, key_rows, preferred_element_type=jnp.float32)
        * head_scale
    )
    distance = query_pos[:, None] - key_pos[None, :]
    steps = (distance[:, :, None] >= rise_points[None, None, :]).astype(jnp.float32)
    pair_bias = jnp.einsum("hb,qkb->hqk", table_step, steps, precision=lax.Precision.HIGHEST)
    allowed = (distance >= 0)[None, :, :] & (key_pos[None, None, :] < lengths[:, None, None])
    logits = jnp.where(allowed[:, None], scores + pair_bias[None], masked_value)
    return (logits, steps)


def on_device(
    tokens,
    lengths,
    expert_ids,
    places,
    buckets,
    w_attn,
    bias_table,
    norm1_gain,
    norm2_gain,
    w_router,
    w_gate,
    w_up,
    w_down,
    cotangent,
):
    span_rows, pair_count, model_width = tokens.shape
    head_count, bucket_count = bias_table.shape
    head_size = model_width // head_count
    head_scale = head_size ** (-0.5)
    n_cp = lax.axis_size("cp")
    n_ep = lax.axis_size("ep")
    seq_len = span_rows * n_cp
    row_count = span_rows * pair_count
    top_count = expert_ids.shape[2]
    experts = w_router.shape[1]
    exp_dev = w_gate.shape[0]
    capacity = (5 * row_count * top_count + 4 * experts - 1) // (4 * experts)
    my_start = lax.axis_index("cp") * span_rows
    query_pos = my_start + jnp.arange(span_rows, dtype=jnp.int32)
    live_mask = (query_pos[:, None] < lengths[None, :]).astype(jnp.float32)
    inputs = tokens.astype(jnp.float32)
    scale_first = root_scale(inputs)
    normed_first = (inputs * scale_first * norm1_gain).astype(jnp.bfloat16)
    w_qkv = w_attn[:, : 3 * model_width]
    w_out = w_attn[:, 3 * model_width :]
    qkv = jnp.einsum("csd,de->cse", normed_first, w_qkv, preferred_element_type=jnp.float32).astype(
        jnp.bfloat16
    )
    queries = qkv[..., :model_width].reshape(span_rows, pair_count, head_count, head_size)
    keyval = qkv[..., model_width:]
    keyval_all = lax.all_gather(keyval, "cp", axis=0, tiled=True)
    bucket_ids = jnp.arange(bucket_count, dtype=jnp.int32)
    rise_points = jnp.sum((buckets[:, None] < bucket_ids[None, :]).astype(jnp.int32), axis=0)
    table_step = jnp.concatenate(
        [bias_table[:, :1], bias_table[:, 1:] - bias_table[:, :-1]], axis=1
    )
    block_starts = jnp.arange(n_cp, dtype=jnp.int32) * span_rows

    def split_kv(kv_block):
        key_rows = kv_block[..., :model_width].reshape(span_rows, pair_count, head_count, head_size)
        value_rows = kv_block[..., model_width:].reshape(
            span_rows, pair_count, head_count, head_size
        )
        return (key_rows, value_rows)

    kv_blocks = keyval_all.reshape(n_cp, span_rows, pair_count, 2 * model_width)

    def max_step(state_pair, block_item):
        row_peak, row_total = state_pair
        kv_block, block_start = block_item
        key_rows, value_rows = split_kv(kv_block)
        logits, steps = block_logits(
            queries, key_rows, block_start, query_pos, lengths, table_step, rise_points, head_scale
        )
        new_peak = jnp.maximum(row_peak, jnp.max(logits, axis=-1))
        row_total = row_total * jnp.exp(row_peak - new_peak) + jnp.sum(
            jnp.exp(logits - new_peak[..., None]), axis=-1
        )
        return ((new_peak, row_total), None)

    stat_shape = (pair_count, head_count, span_rows)
    (row_peak, row_total), unused = lax.scan(
        max_step,
        (jnp.full(stat_shape, masked_value, jnp.float32), jnp.zeros(stat_shape, jnp.float32)),
        (kv_blocks, block_starts),
    )
    log_total = row_peak + jnp.log(row_total)

    def value_step(running, block_item):
        kv_block, block_start = block_item
        key_rows, value_rows = split_kv(kv_block)
        logits, steps = block_logits(
            queries, key_rows, block_start, query_pos, lengths, table_step, rise_points, head_scale
        )
        weights = jnp.exp(logits - log_total[..., None]).astype(jnp.bfloat16)
        return (
            running
            + jnp.einsum(
                "shqk,kshd->qshd", weights, value_rows, preferred_element_type=jnp.float32
            ),
            None,
        )

    attended, unused = lax.scan(
        value_step,
        jnp.zeros((span_rows, pair_count, head_count, head_size), jnp.float32),
        (kv_blocks, block_starts),
    )
    attended = attended.reshape(span_rows, pair_count, model_width)
    attended_low = attended.astype(jnp.bfloat16)
    projected = jnp.einsum("csd,de->cse", attended_low, w_out, preferred_element_type=jnp.float32)
    hidden = inputs + live_mask[..., None] * projected
    scale_second = root_scale(hidden)
    normed_second = (hidden * scale_second * norm2_gain).astype(jnp.bfloat16)
    router_logits = jnp.einsum(
        "csd,de->cse", normed_second, w_router, preferred_element_type=jnp.float32
    )
    router_probs = jax.nn.softmax(router_logits, axis=-1)
    expert_hot = (expert_ids[..., None] == jnp.arange(experts, dtype=jnp.int32)).astype(jnp.float32)
    kept_mask = (places >= 0).astype(jnp.float32)
    gate_values = jnp.sum(expert_hot * router_probs[:, :, None, :], axis=-1) * kept_mask
    target = jnp.where(places >= 0, expert_ids * capacity + places, -1).reshape(
        row_count, top_count
    )
    slot_ids = jnp.arange(experts * capacity, dtype=jnp.int32)
    route_hot = (target[None, :, :] == slot_ids[:, None, None]).astype(jnp.bfloat16)
    dispatch = jnp.sum(route_hot, axis=2)
    sent_rows = jnp.dot(
        dispatch, normed_second.reshape(row_count, model_width), preferred_element_type=jnp.float32
    )
    sent_rows = sent_rows.astype(jnp.bfloat16).reshape(n_ep, exp_dev, capacity, model_width)
    arrived = lax.all_to_all(sent_rows, "ep", split_axis=0, concat_axis=0, tiled=True)
    gate_pre = jnp.einsum("secd,edf->secf", arrived, w_gate, preferred_element_type=jnp.float32)
    up_pre = jnp.einsum("secd,edf->secf", arrived, w_up, preferred_element_type=jnp.float32)
    active, gelu_pullback = jax.vjp(gelu_tanh, gate_pre)
    inner_act = (active * up_pre).astype(jnp.bfloat16)
    produced = jnp.einsum(
        "secf,edf->secd", inner_act, w_down, preferred_element_type=jnp.float32
    ).astype(jnp.bfloat16)
    returned = lax.all_to_all(produced, "ep", split_axis=0, concat_axis=0, tiled=True).reshape(
        experts * capacity, model_width
    )
    picked = jnp.einsum("jrk,jd->rkd", route_hot, returned, preferred_element_type=jnp.float32)
    gate_flat = gate_values.reshape(row_count, top_count)
    mixed = hidden.reshape(row_count, model_width) + jnp.sum(gate_flat[..., None] * picked, axis=1)
    mixed = mixed.reshape(span_rows, pair_count, model_width).astype(jnp.bfloat16)
    grad_out = cotangent.astype(jnp.float32).reshape(row_count, model_width)
    gate_grads = jnp.sum(grad_out[:, None, :] * picked, axis=-1)
    sent_back = (gate_flat[..., None] * grad_out[:, None, :]).astype(jnp.bfloat16)
    scattered = jnp.einsum("jrk,rkd->jd", route_hot, sent_back, preferred_element_type=jnp.float32)
    scattered = scattered.astype(jnp.bfloat16).reshape(n_ep, exp_dev, capacity, model_width)
    grad_produced = lax.all_to_all(scattered, "ep", split_axis=0, concat_axis=0, tiled=True)
    down_grad = jnp.einsum(
        "secd,secf->edf", grad_produced, inner_act, preferred_element_type=jnp.float32
    )
    grad_inner = jnp.einsum(
        "secd,edf->secf", grad_produced, w_down, preferred_element_type=jnp.float32
    )
    grad_gate_pre = gelu_pullback(grad_inner * up_pre)[0].astype(jnp.bfloat16)
    grad_up_pre = (grad_inner * active).astype(jnp.bfloat16)
    gate_grad = jnp.einsum(
        "secd,secf->edf", arrived, grad_gate_pre, preferred_element_type=jnp.float32
    )
    up_grad = jnp.einsum("secd,secf->edf", arrived, grad_up_pre, preferred_element_type=jnp.float32)
    grad_arrived = jnp.einsum(
        "secf,edf->secd", grad_gate_pre, w_gate, preferred_element_type=jnp.float32
    )
    grad_arrived = (
        grad_arrived
        + jnp.einsum("secf,edf->secd", grad_up_pre, w_up, preferred_element_type=jnp.float32)
    ).astype(jnp.bfloat16)
    grad_sent = lax.all_to_all(grad_arrived, "ep", split_axis=0, concat_axis=0, tiled=True).reshape(
        experts * capacity, model_width
    )
    grad_rows = jnp.einsum("jr,jd->rd", dispatch, grad_sent, preferred_element_type=jnp.float32)
    choice_grads = gate_grads.reshape(span_rows, pair_count, top_count) * kept_mask
    prob_grads = jnp.sum(expert_hot * choice_grads[..., None], axis=2)
    logit_grads = router_probs * (
        prob_grads - jnp.sum(router_probs * prob_grads, axis=-1, keepdims=True)
    )
    logit_grads = logit_grads.astype(jnp.bfloat16)
    router_grad = jnp.einsum(
        "csd,cse->de", normed_second, logit_grads, preferred_element_type=jnp.float32
    )
    grad_normed_second = grad_rows.reshape(span_rows, pair_count, model_width)
    grad_normed_second = grad_normed_second + jnp.einsum(
        "cse,de->csd", logit_grads, w_router, preferred_element_type=jnp.float32
    )
    gain_second_grad = jnp.sum(grad_normed_second * hidden * scale_second, axis=(0, 1))
    grad_hidden = grad_out.reshape(span_rows, pair_count, model_width) + norm_back(
        grad_normed_second, hidden, scale_second, norm2_gain
    )
    grad_proj = (live_mask[..., None] * grad_hidden).astype(jnp.bfloat16)
    out_grad = jnp.einsum(
        "csd,cse->de", attended_low, grad_proj, preferred_element_type=jnp.float32
    )
    grad_att = jnp.einsum(
        "cse,de->csd", grad_proj, w_out, preferred_element_type=jnp.float32
    ).astype(jnp.bfloat16)
    grad_att_heads = grad_att.reshape(span_rows, pair_count, head_count, head_size)
    row_terms = jnp.sum(
        grad_att_heads.astype(jnp.float32)
        * attended.reshape(span_rows, pair_count, head_count, head_size),
        axis=-1,
    )
    row_terms = row_terms.transpose(1, 2, 0)
    keyval_back = lax.all_gather(keyval, "cp", axis=0, tiled=True)
    back_blocks = keyval_back.reshape(n_cp, span_rows, pair_count, 2 * model_width)

    def pair_terms(
        query_rows, grad_rows_att, row_part, total_part, key_rows, value_rows, key_start, rows_pos
    ):
        logits, steps = block_logits(
            query_rows, key_rows, key_start, rows_pos, lengths, table_step, rise_points, head_scale
        )
        weights = jnp.exp(logits - total_part[..., None])
        weight_grads = jnp.einsum(
            "qshd,kshd->shqk", grad_rows_att, value_rows, preferred_element_type=jnp.float32
        )
        score_grads = weights * (weight_grads - row_part[..., None])
        return (weights, score_grads, steps)

    def query_side_step(state_pair, kv_block, block_start):
        query_grad, step_grad = state_pair
        key_rows, value_rows = split_kv(kv_block)
        weights, score_grads, steps = pair_terms(
            queries,
            grad_att_heads,
            row_terms,
            log_total,
            key_rows,
            value_rows,
            block_start,
            query_pos,
        )
        low_grads = score_grads.astype(jnp.bfloat16)
        query_grad = (
            query_grad
            + jnp.einsum("shqk,kshd->qshd", low_grads, key_rows, preferred_element_type=jnp.float32)
            * head_scale
        )
        step_grad = step_grad + jnp.einsum(
            "hqk,qkb->hb", jnp.sum(score_grads, axis=0), steps, precision=lax.Precision.HIGHEST
        )
        return ((query_grad, step_grad), weights, low_grads)

    start_state = (
        jnp.zeros((span_rows, pair_count, head_count, head_size), jnp.float32),
        jnp.zeros((head_count, bucket_count), jnp.float32),
    )

    def grad_step(state_pair, block_item):
        kv_block, block_start = block_item
        new_state, weights, low_grads = query_side_step(state_pair, kv_block, block_start)
        value_grad = jnp.einsum(
            "shqk,qshd->kshd",
            weights.astype(jnp.bfloat16),
            grad_att_heads,
            preferred_element_type=jnp.float32,
        )
        key_grad = (
            jnp.einsum("shqk,qshd->kshd", low_grads, queries, preferred_element_type=jnp.float32)
            * head_scale
        )
        block_grad = jnp.concatenate(
            [
                key_grad.reshape(span_rows, pair_count, model_width),
                value_grad.reshape(span_rows, pair_count, model_width),
            ],
            axis=-1,
        )
        return (new_state, block_grad)

    (query_grad, step_grad), kv_terms = lax.scan(
        grad_step, start_state, (back_blocks, block_starts)
    )
    kv_terms = kv_terms.reshape(seq_len, pair_count, 2 * model_width)
    keyval_grad = lax.psum_scatter(
        kv_terms.astype(jnp.bfloat16), "cp", scatter_dimension=0, tiled=True
    )
    table_grad = step_grad - jnp.concatenate(
        [step_grad[:, 1:], jnp.zeros((head_count, 1), jnp.float32)], axis=1
    )
    qkv_grad = jnp.concatenate(
        [query_grad.reshape(span_rows, pair_count, model_width).astype(jnp.bfloat16), keyval_grad],
        axis=-1,
    )
    qkv_weight_grad = jnp.einsum(
        "csd,cse->de", normed_first, qkv_grad, preferred_element_type=jnp.float32
    )
    grad_normed_first = jnp.einsum(
        "cse,de->csd", qkv_grad, w_qkv, preferred_element_type=jnp.float32
    )
    gain_first_grad = jnp.sum(grad_normed_first * inputs * scale_first, axis=(0, 1))
    tokens_grad = (
        grad_hidden + norm_back(grad_normed_first, inputs, scale_first, norm1_gain)
    ).astype(jnp.bfloat16)
    attn_term = jnp.concatenate([qkv_weight_grad, out_grad], axis=1)
    w_attn_grad = lax.psum_scatter(attn_term, ("dp", "ep", "cp"), scatter_dimension=1, tiled=True)
    router_sum, table_sum, gain_first_sum, gain_second_sum = lax.psum(
        (router_grad, table_grad, gain_first_grad, gain_second_grad), ("dp", "ep", "cp")
    )
    gate_sum, up_sum, down_sum = (
        lax.psum_scatter(
            gate_grad.astype(jnp.bfloat16), ("dp", "cp"), scatter_dimension=2, tiled=True
        ).astype(jnp.float32),
        lax.psum_scatter(
            up_grad.astype(jnp.bfloat16), ("dp", "cp"), scatter_dimension=2, tiled=True
        ).astype(jnp.float32),
        lax.psum_scatter(
            down_grad.astype(jnp.bfloat16), ("dp", "cp"), scatter_dimension=2, tiled=True
        ).astype(jnp.float32),
    )
    return (
        mixed,
        tokens_grad,
        w_attn_grad,
        table_sum,
        gain_first_sum,
        gain_second_sum,
        router_sum,
        gate_sum,
        up_sum,
        down_sum,
    )


minus_big = -1000000000.0
vmem_bytes = 60 * 1024 * 1024


cost_share = 0.05


def cost(flops, moved):
    return pl.CostEstimate(
        flops=int(flops * cost_share), bytes_accessed=int(moved * cost_share), transcendentals=0
    )


def held(kernel, at, count):
    def run(*refs):
        kernel(*refs[:at], *refs[at + count :])

    return run


def anywhere(arrays):
    return [pl.BlockSpec(memory_space=pl.ANY)] * len(arrays)


def compiler_params():
    return pltpu.CompilerParams(vmem_limit_bytes=vmem_bytes)


def shear(values, leftward):
    rows, lanes = values.shape
    row_ids = lax.broadcasted_iota(jnp.int32, (rows, lanes), 0)
    bit = 1
    while bit < rows:
        amount = lanes - bit if leftward else bit
        moved = pltpu.roll(values, amount, 1)
        values = jnp.where((row_ids & bit) != 0, moved, values)
        bit *= 2
    return values


def dot_nt(left, right):
    return lax.dot_general(
        left, right, (((1,), (1,)), ((), ())), preferred_element_type=jnp.float32
    )


def dot_tn(left, right):
    return lax.dot_general(
        left, right, (((0,), (0,)), ((), ())), preferred_element_type=jnp.float32
    )


def dot_nn(left, right):
    return jnp.dot(left, right, preferred_element_type=jnp.float32)


def key_masks(length, blocks, span_rows):
    masks = []
    for block in range(blocks):
        position = block * span_rows + lax.broadcasted_iota(jnp.int32, (1, span_rows), 1)
        masks.append(jnp.where(position < length, 0.0, minus_big))
    return masks


def forward_body(
    mine, length, scale, head_size, qkv_ref, bias_ref, low_ref, full_ref, total_ref, after_pair
):
    blocks, span_rows, width = qkv_ref.shape
    lanes = 128
    lane = lax.broadcasted_iota(jnp.int32, (1, lanes), 1)
    masks = key_masks(length, blocks, span_rows)
    halves = lanes // head_size

    def place(block):
        return lax.rem(mine - block + blocks, blocks)

    def one_pair(pair, carry):
        wide = pl.multiple_of(pair * (3 * lanes), lanes)
        own_lanes = pl.ds(pl.multiple_of(pair * lanes, lanes), lanes)
        part = [pl.ds(pl.multiple_of(wide + which * lanes, lanes), lanes) for which in range(3)]
        for row in range(blocks):
            queries = qkv_ref[place(row), :, part[0]]
            totals = jnp.zeros((span_rows, lanes), jnp.float32)
            result = jnp.zeros((span_rows, lanes), jnp.float32)
            for half in range(halves):
                own = lane // head_size == half
                head_q = queries * jnp.where(own, scale, 0.0).astype(jnp.bfloat16)
                head_v = jnp.where(own, 1.0, 0.0).astype(jnp.bfloat16)
                logits = []
                for column in range(row + 1):
                    at = (blocks - 1 - row + column) * span_rows
                    term = dot_nt(head_q, qkv_ref[place(column), :, part[1]])
                    bias = bias_ref[pair * halves + half, :, at : at + span_rows]
                    logits.append(term + bias + masks[column])
                peak = jnp.max(logits[0], axis=1, keepdims=True)
                for term in logits[1:]:
                    peak = jnp.maximum(peak, jnp.max(term, axis=1, keepdims=True))
                total = jnp.zeros((span_rows, 1), jnp.float32)
                mixed = jnp.zeros((span_rows, lanes), jnp.float32)
                for column in range(row + 1):
                    weights = jnp.exp(logits[column] - peak)
                    total = total + jnp.sum(weights, axis=1, keepdims=True)
                    values = qkv_ref[place(column), :, part[2]] * head_v
                    mixed = mixed + dot_nn(weights.astype(jnp.bfloat16), values)
                result = result + mixed / total
                totals = jnp.where(lane == half, peak + jnp.log(total), totals)
            low_ref[place(row), :, own_lanes] = result.astype(jnp.bfloat16)
            full_ref[row, :, own_lanes] = result
            total_ref[row, :, own_lanes] = totals
        after_pair(pair)
        return carry

    lax.fori_loop(0, width // (3 * lanes), one_pair, 0)


def backward_body(
    mine, length, scale, head_size, qkv_ref, bias_ref, grad_ref, full_ref, total_ref, ring_ref, line_ref, work,
    after_pair=None,
):
    key_sum, value_sum, plane = work
    blocks, span_rows, width = qkv_ref.shape
    lanes = 128
    lane = lax.broadcasted_iota(jnp.int32, (1, lanes), 1)
    masks = key_masks(length, blocks, span_rows)
    halves = lanes // head_size

    def place(block):
        return lax.rem(mine - block + blocks, blocks)

    def one_pair(pair, carry):
        wide = pl.multiple_of(pair * (3 * lanes), lanes)
        own_lanes = pl.ds(pl.multiple_of(pair * lanes, lanes), lanes)
        part = [pl.ds(pl.multiple_of(wide + which * lanes, lanes), lanes) for which in range(3)]
        key_sum[...] = jnp.zeros_like(key_sum)
        value_sum[...] = jnp.zeros_like(value_sum)
        plane[...] = jnp.zeros_like(plane)
        for row in range(blocks):
            queries = qkv_ref[place(row), :, part[0]]
            grads = grad_ref[lax.rem(row - mine + blocks, blocks), :, own_lanes]
            products = grads.astype(jnp.float32) * full_ref[row, :, own_lanes]
            totals = total_ref[row, :, own_lanes]
            query_sum = jnp.zeros((span_rows, lanes), jnp.float32)
            for half in range(halves):
                own = lane // head_size == half
                one = jnp.where(own, 1.0, 0.0).astype(jnp.bfloat16)
                head_q = queries * jnp.where(own, scale, 0.0).astype(jnp.bfloat16)
                head_g = grads * one
                delta = jnp.sum(jnp.where(own, products, 0.0), axis=1, keepdims=True)
                total = totals[:, half : half + 1]
                for column in range(row + 1):
                    at = (blocks - 1 - row + column) * span_rows
                    keys = qkv_ref[place(column), :, part[1]]
                    logits = dot_nt(head_q, keys)
                    bias = bias_ref[pair * halves + half, :, at : at + span_rows]
                    logits = logits + bias + masks[column]
                    weights = jnp.exp(logits - total)
                    weight_grads = dot_nt(head_g, qkv_ref[place(column), :, part[2]])
                    score_grads = weights * (weight_grads - delta)
                    plane[half, :, at : at + span_rows] += score_grads
                    low_weights = weights.astype(jnp.bfloat16)
                    low_grads = score_grads.astype(jnp.bfloat16)
                    query_sum = query_sum + dot_nn(low_grads, keys * one)
                    key_sum[column] += dot_tn(low_grads, head_q)
                    value_sum[column] += dot_tn(low_weights, head_g)
            ring_ref[place(row), :, part[0]] = (query_sum * scale).astype(jnp.bfloat16)
        for row in range(blocks):
            ring_ref[place(row), :, part[1]] = key_sum[row].astype(jnp.bfloat16)
            ring_ref[place(row), :, part[2]] = value_sum[row].astype(jnp.bfloat16)
        for half in range(halves):
            full = jnp.concatenate(
                [plane[half], jnp.zeros((span_rows, span_rows), jnp.float32)], axis=1
            )
            summed = jnp.sum(shear(full, True), axis=0, keepdims=True)
            line_ref[pair * halves + half] = pltpu.roll(summed, span_rows - 1, 1)
        if after_pair is not None:
            after_pair(pair)
        return carry

    lax.fori_loop(0, width // (3 * lanes), one_pair, 0)


def backward_work(blocks, span_rows, head_size):
    return [
        pltpu.VMEM((blocks, span_rows, 128), jnp.float32),
        pltpu.VMEM((blocks, span_rows, 128), jnp.float32),
        pltpu.VMEM((128 // head_size, span_rows, blocks * span_rows), jnp.float32),
    ]


def greet(*others):
    barrier = pltpu.get_barrier_semaphore()
    for other in others:
        pl.semaphore_signal(
            barrier, inc=1, device_id=other, device_id_type=pl.DeviceIdType.MESH
        )
    pl.semaphore_wait(barrier, len(others))


def push(source, target, send_sem, recv_sem, other):
    return pltpu.make_async_remote_copy(
        src_ref=source,
        dst_ref=target,
        send_sem=send_sem,
        recv_sem=recv_sem,
        device_id=other,
        device_id_type=pl.DeviceIdType.MESH,
    )


def ring_others(mine, count):
    return [{"cp": lax.rem(mine + j, count)} for j in range(1, count)]


def slot_of(ref, slot, slots):
    width = ref.shape[1] // slots
    return ref.at[:, pl.ds(slot * width, width)]


def deliveries(source, target, sems, mine, count, lanes=None):
    return [
        push(
            source.at[j] if lanes is None else source.at[j, :, lanes],
            target.at[j],
            sems.at[0, j],
            sems.at[1, j],
            {"cp": lax.rem(mine + (count - j), count)},
        )
        for j in range(1, count)
    ]


def remote_params(number):
    return pltpu.CompilerParams(
        vmem_limit_bytes=vmem_bytes, collective_id=number, has_side_effects=True
    )


def own_rows(block, length, span_rows):
    position = block * span_rows + lax.broadcasted_iota(jnp.int32, (span_rows, 1), 0)
    return jnp.where(position < length, 1.0, 0.0)


def router_of(rows, router_w, experts):
    lane = lax.broadcasted_iota(jnp.int32, (1, router_w.shape[1]), 1)
    logits = jnp.where(lane < experts, dot_nn(rows, router_w), minus_big)
    shares = jnp.exp(logits - jnp.max(logits, axis=1, keepdims=True))
    return shares / jnp.sum(shares, axis=1, keepdims=True)


def project_body(mine, length, input_ref, gain_ref, weight_ref, parts_ref, own_ref, attended_ref, hidden_ref, normed_ref):
    count, span_rows, width = parts_ref.shape
    for j in range(count):
        owner = lax.rem(mine + j, count)
        for group in range(width // 128):
            at = pl.multiple_of((group * count + owner) * 128, 128)
            lanes = slice(group * 128, (group + 1) * 128)
            attended_ref[:, pl.ds(at, 128)] = own_ref[0, :, lanes] if j == 0 else parts_ref[j, :, lanes]
    projected = dot_nn(attended_ref[...], weight_ref[...])
    hidden = input_ref[...].astype(jnp.float32) + own_rows(mine, length, span_rows) * projected
    hidden_ref[...] = hidden
    normed_ref[...] = (hidden * root_scale(hidden) * gain_ref[...]).astype(jnp.bfloat16)


def pick_body(base, capacity, experts, chosen, parts, out_ref):
    for expert in range(experts):
        picked = None
        for choice_ref, part in zip(chosen, parts):
            span = part.shape[0]
            ids = lax.broadcasted_iota(jnp.int32, (capacity, span), 0) + (base + expert * capacity)
            hot = jnp.zeros((capacity, span), jnp.float32)
            for choice in range(choice_ref.shape[0]):
                hot = hot + jnp.where(ids == choice_ref[choice : choice + 1, :], 1.0, 0.0)
            term = dot_nn(hot.astype(jnp.bfloat16), part[...])
            picked = term if picked is None else picked + term
        out_ref[expert] = picked.astype(jnp.bfloat16)


def front_kernel(
    scale, head_size, slots, length_ref, gain_first_ref, gain_second_ref, line_ref, target_ref, w_attn_ref, weight_ref,
    tokens_ref, cotangent_ref, *refs
):
    inputs = [slot_of(tokens_ref, s, slots) for s in range(slots)]
    grads = [slot_of(cotangent_ref, s, slots) for s in range(slots)]
    stores_to, own_w, targets_ref = refs[:5], refs[5], refs[6]
    over_ref, up_ref = refs[7:9]
    picks = [refs[9 + 2 * i : 11 + 2 * i] for i in range(3)]
    outs = [refs[15 + 3 * s : 18 + 3 * s] for s in range(slots)]
    refs = refs[15 + 3 * slots :]
    low, arrived, near_grads, ring_sems, own_sems, give_sems, plane_sems, target_sems = refs[:8]
    core_sems, normed_sems, store_sems, *made = refs[8:]
    all_ref, qkv_ref, bias_ref, full_ref, total_ref = made
    _, count, span_rows, model_width = all_ref.shape

    def store(which, slot):
        source, target = made[which], stores_to[which]
        if which != 2:
            source, target = source.at[slot], target.at[slot]
        return pltpu.make_async_copy(source, target, store_sems.at[which, slot])

    groups = own_w.shape[1] // 384
    mine = lax.axis_index("cp")
    dp, ep = lax.axis_index("dp"), lax.axis_index("ep")
    core_other, x_other, y_other = near_others(dp, ep)

    loads = []
    for group in range(groups):
        for which in range(3):
            at = which * model_width + (group * count + mine) * 128
            lanes = pl.ds((group * 3 + which) * 128, 128)
            loads.append(
                pltpu.make_async_copy(
                    w_attn_ref.at[:, pl.ds(pl.multiple_of(at, 128), 128)],
                    own_w.at[:, lanes],
                    own_sems.at[group * 3 + which],
                )
            )
    for load in loads:
        load.start()
    for s in range(slots):
        values = inputs[s][...].astype(jnp.float32)
        all_ref[s, 0] = (values * root_scale(values) * gain_first_ref[...]).astype(jnp.bfloat16)
    greet(*ring_others(mine, count), core_other, x_other, y_other)

    def hop_copy(slot, hop):
        return push(
            all_ref.at[slot, hop],
            all_ref.at[slot, hop + 1],
            ring_sems.at[0, slot, hop],
            ring_sems.at[1, slot, hop],
            {"cp": lax.rem(mine + 1, count)},
        )

    for s in range(slots):
        hop_copy(s, 0).start()

    def plane_copies(source, target, sems):
        first = [
            push(source(s), target.at[way, s], sems.at[0, way, s], sems.at[1, way, s], other)
            for s in (0, 1)
            for way, other in ((0, x_other), (1, y_other))
        ]
        second = [
            push(target.at[0, 0], target.at[2, 0], sems.at[0, 2, 0], sems.at[1, 2, 0], y_other),
            push(target.at[1, 1], target.at[2, 1], sems.at[0, 2, 1], sems.at[1, 2, 1], x_other),
        ]
        return first, second

    grad_first, grad_second = plane_copies(lambda s: grads[s], near_grads, plane_sems)
    near_targets = targets_ref.at[pl.ds(1, 3)]
    place_first, place_second = plane_copies(lambda s: target_ref.at[s], near_targets, target_sems)
    for copy in place_first + grad_first:
        copy.start()
    targets_ref[0] = target_ref[...]
    for load in loads:
        load.wait()
    for s in range(slots):
        qkv_ref[s, 0] = dot_nn(all_ref[s, 0], own_w[...]).astype(jnp.bfloat16)
    columns = bias_ref.shape[2]
    lanes = span_rows + columns
    for head in range(bias_ref.shape[0]):
        line = pltpu.roll(line_ref[head], lanes - (span_rows - 1), 1)
        full = jnp.broadcast_to(line, (span_rows, lanes))
        bias_ref[head] = shear(full, False)[:, :columns]
    store(2, 0).start()

    _, experts, capacity, _ = picks[0][0].shape
    base = ep * (experts * capacity)
    at_of = ((0, 0), (1, 0), (1, 1), (1, 2), (2, 0))

    def pick(source):
        if source == 0:
            parts = grads
        elif source == 4:
            parts = [outs[s][2] for s in range(slots)]
        else:
            parts = [near_grads.at[source - 1, s] for s in range(slots)]
        chosen = [targets_ref.at[source % 4, s] for s in range(slots)]
        group, at = at_of[source]
        pick_body(base, capacity, experts, chosen, parts, picks[group][0].at[at])
        core_copy(source).start()

    def core_copy(source):
        group, at = at_of[source]
        return push(
            picks[group][0].at[at],
            picks[group][1].at[at],
            core_sems.at[0, source],
            core_sems.at[1, source],
            core_other,
        )

    def normed_copy(at):
        source, target, other = (
            (outs[0][2], over_ref, x_other),
            (outs[0][2], up_ref, y_other),
        )[at]
        return push(source, target, normed_sems.at[0, at], normed_sems.at[1, at], other)

    def project(slot):
        for pair in range(groups):
            for copy in gives(slot, pair):
                copy.wait()
        project_body(
            mine, length_ref[slot], inputs[slot], gain_second_ref, weight_ref, arrived.at[slot],
            low.at[slot], *outs[slot],
        )

    def gives(slot, pair):
        part = pl.ds(pl.multiple_of(pair * 128, 128), 128)
        return [
            push(
                low.at[slot, j, :, part],
                arrived.at[slot, j, :, part],
                give_sems.at[0, slot, pair, j],
                give_sems.at[1, slot, pair, j],
                {"cp": lax.rem(mine + (count - j), count)},
            )
            for j in range(1, count)
        ]

    def attend(slot):
        def after_pair(pair):
            for copy in gives(slot, pair):
                copy.start()

        forward_body(
            mine, length_ref[slot], scale, head_size, qkv_ref.at[slot], bias_ref, low.at[slot],
            full_ref.at[slot], total_ref.at[slot], after_pair,
        )
        for which in (0, 1, 3, 4):
            store(which, slot).start()

    pick(0)
    for hop in range(1, count):
        for s in range(slots):
            hop_copy(s, hop - 1).wait_recv()
            if hop < count - 1:
                hop_copy(s, hop).start()
            qkv_ref[s, hop] = dot_nn(all_ref[s, hop], own_w[...]).astype(jnp.bfloat16)
            if hop == count - 1 and s + 1 < slots:
                attend(s)
        if hop == 1:
            for copy in place_first + grad_first:
                copy.wait_recv()
            for copy in place_second + grad_second:
                copy.start()
            pick(1)
            pick(2)
        if hop == 2:
            for copy in place_second + grad_second:
                copy.wait_recv()
            pick(3)
    attend(slots - 1)
    project(0)
    for at in range(2):
        normed_copy(at).start()
    project(1)
    pick(4)
    for s in range(slots):
        for hop in range(count - 1):
            hop_copy(s, hop).wait_send()
    for copy in place_first + grad_first + place_second + grad_second:
        copy.wait_send()
    for at in range(2):
        normed_copy(at).wait()
    for source in range(5):
        core_copy(source).wait()
    store(2, 0).wait()
    for s in range(slots):
        for which in (0, 1, 3, 4):
            store(which, s).wait()


def front(lengths, gain_first, gain_second, lines, target, w_attn, inputs, grads, slots, count, experts, capacity, scale, head_size):
    span_rows, model_width = inputs.shape[0], inputs.shape[1] // slots
    heads, _, lanes = lines.shape
    own_width = 3 * model_width // count
    groups = own_width // 384
    choices = target.shape[1]
    whole = pl.BlockSpec(memory_space=pltpu.VMEM)
    f32, bf16 = jnp.float32, jnp.bfloat16
    shape = jax.ShapeDtypeStruct
    made = (
        ((slots, count, span_rows, model_width), bf16),
        ((slots, count, span_rows, own_width), bf16),
        ((heads, span_rows, lanes - span_rows), f32),
        ((slots, count, span_rows, groups * 128), f32),
        ((slots, count, span_rows, groups * 128), f32),
    )
    got = pl.pallas_call(
        functools.partial(front_kernel, scale, head_size, slots),
        grid=(1,),
        in_specs=[
            pl.BlockSpec(memory_space=pltpu.SMEM),
            whole,
            whole,
            whole,
            whole,
            pl.BlockSpec(memory_space=pl.ANY),
            pl.BlockSpec((model_width, model_width), lambda i: (0, 3)),
            whole,
            whole,
        ],
        out_specs=[pl.BlockSpec(memory_space=pl.ANY)] * 5 + [whole] * (10 + 3 * slots),
        out_shape=[
            *(shape(*kind) for kind in made),
            shape((model_width, own_width), bf16),
            shape((4, slots, choices, span_rows), jnp.int32),
        ]
        + [shape((span_rows, model_width), bf16)] * 2
        + [
            shape((sources, experts, capacity, model_width), bf16)
            for sources in (1, 3, 1)
            for _ in range(2)
        ]
        + [
            shape((span_rows, model_width), bf16),
            shape((span_rows, model_width), f32),
            shape((span_rows, model_width), bf16),
        ]
        * slots,
        scratch_shapes=[
            pltpu.VMEM((slots, count, span_rows, groups * 128), bf16),
            pltpu.VMEM((slots, count, span_rows, groups * 128), bf16),
            pltpu.VMEM((3, slots, span_rows, model_width), bf16),
            pltpu.SemaphoreType.DMA((2, slots, count - 1)),
            pltpu.SemaphoreType.DMA((3 * groups,)),
            pltpu.SemaphoreType.DMA((2, slots, groups, count)),
            pltpu.SemaphoreType.DMA((2, 3, slots)),
            pltpu.SemaphoreType.DMA((2, 3, slots)),
            pltpu.SemaphoreType.DMA((2, 5)),
            pltpu.SemaphoreType.DMA((2, 3)),
            pltpu.SemaphoreType.DMA((5, slots)),
            *(pltpu.VMEM(*kind) for kind in made),
        ],
        cost_estimate=cost(60e9, 20e6),
        compiler_params=remote_params(0),
        name="front",
    )(lengths, gain_first, gain_second, lines, target, w_attn, w_attn, inputs, grads)
    pairs = [got[9 + 2 * i : 11 + 2 * i] for i in range(3)]
    return got[:9], pairs, [got[15 + 3 * s : 18 + 3 * s] for s in range(slots)]


def hidden_body(
    experts, mine, length, back_ref, grad_ref, hidden_ref, normed_ref, gain_ref, router_ref, weight_ref,
    hidden_grad_ref, proj_ref, router_grad_ref, gain_grad_ref, leaving_ref, attended,
):
    count = leaving_ref.shape[0]
    span_rows, model_width = hidden_ref.shape
    back = back_ref[...]
    normed = normed_ref[...]
    probs = router_of(normed, router_ref[...], experts)
    shares = back[:, model_width:]
    logit_grads = probs * (shares - jnp.sum(probs * shares, axis=1, keepdims=True))
    logit_grads = logit_grads.astype(jnp.bfloat16)
    router_grad_ref[...] = dot_tn(normed, logit_grads)
    grads = back[:, :model_width] + dot_nt(logit_grads, router_ref[...])
    hidden = hidden_ref[...]
    scale_rows = root_scale(hidden)
    gain_grad_ref[...] = jnp.sum(grads * hidden * scale_rows, axis=0, keepdims=True)
    hidden_grads = grad_ref[...].astype(jnp.float32) + norm_back(
        grads, hidden, scale_rows, gain_ref[...]
    )
    hidden_grad_ref[...] = hidden_grads
    proj = (own_rows(mine, length, span_rows) * hidden_grads).astype(jnp.bfloat16)
    proj_ref[...] = proj
    attended[...] = dot_nt(proj, weight_ref[...]).astype(jnp.bfloat16)
    for j in range(count):
        owner = lax.rem(mine + (count - j), count)
        for group in range(leaving_ref.shape[2] // 128):
            at = pl.multiple_of((group * count + owner) * 128, 128)
            leaving_ref[j, :, group * 128 : (group + 1) * 128] = attended[:, pl.ds(at, 128)]


def hidden_kernel(
    experts, scale, head_size, slots, length_ref, gain_ref, router_ref, weight_ref, qkv_all, bias_all, full_all, total_all,
    cotangent_ref, *refs
):
    per_slot = [
        (refs[3 * s], slot_of(cotangent_ref, s, slots), *refs[3 * s + 1 : 3 * s + 3])
        for s in range(slots)
    ]
    refs = refs[3 * slots :]
    own_out, rest_out, refs = refs[:slots], refs[slots : 4 * slots], refs[4 * slots :]
    outs = [refs[4 * s : 4 * s + 4] for s in range(slots)]
    mixed, refs = refs[4 * slots : 5 * slots], refs[5 * slots :]
    ring_ref, line_ref, rest_ref, leaving, arriving, attended, sems = refs[:7]
    got, far, last, low, out_sems = refs[7:12]
    qkv_ref, bias_ref, full_ref, total_ref, held_out, load_sems = refs[12:18]
    work = refs[18:]
    count = qkv_ref.shape[0]
    mine = lax.axis_index("cp")
    _, x_other, y_other = near_others(lax.axis_index("dp"), lax.axis_index("ep"))
    over, up, across = (rest_out[i * slots : (i + 1) * slots] for i in range(3))
    loads = [
        pltpu.make_async_copy(source, target, load_sems.at[at])
        for at, (source, target) in enumerate(
            (
                (qkv_all.at[0], qkv_ref),
                (bias_all, bias_ref),
                (full_all.at[0], full_ref),
                (total_all.at[0], total_ref),
                (up[0], held_out.at[0]),
                (over[1], held_out.at[1]),
                (own_out[0], held_out.at[2]),
                (own_out[1], held_out.at[3]),
            )
        )
    ]
    for load in loads:
        load.start()
    greet(*ring_others(mine, count), x_other, y_other)

    def out_copy(at):
        source, target, other = (
            (over[0], got.at[0], x_other),
            (up[1], got.at[1], y_other),
            (across[0], far.at[0], x_other),
            (across[1], far.at[1], y_other),
            (low.at[0], last.at[0], y_other),
            (low.at[1], last.at[1], x_other),
        )[at]
        return push(source, target, out_sems.at[0, at], out_sems.at[1, at], other)

    def after_pair(pair):
        @pl.when(pair == 0)
        def _():
            for at in range(2):
                out_copy(2 + at).wait()
                summed = held_out[at].astype(jnp.float32) + far[at].astype(jnp.float32)
                low[at] = summed.astype(jnp.bfloat16)
                out_copy(4 + at).start()

    for at in (2, 3, 0, 1):
        out_copy(at).start()
    copies = []
    for s in range(slots):
        hidden_body(
            experts, mine, length_ref[s], *per_slot[s], gain_ref, router_ref, weight_ref,
            *outs[s], leaving.at[s], attended,
        )
        target = arriving if s == 0 else rest_ref.at[s - 1]
        copies.append(deliveries(leaving.at[s], target, sems.at[s], mine, count))
        if s == 0:
            for copy in copies[s]:
                copy.start()
        target[0] = leaving[s, 0]
    for copy in copies[0]:
        copy.wait()
    for some in copies[1:]:
        for copy in some:
            copy.start()
    for load in loads:
        load.wait()
    backward_body(
        mine, length_ref[0], scale, head_size, qkv_ref, bias_ref, arriving, full_ref, total_ref,
        ring_ref, line_ref, work, after_pair,
    )
    for s in range(slots):
        out_copy(s).wait()
        out_copy(4 + s).wait()
        home = held_out[2 + s].astype(jnp.float32) + got[s].astype(jnp.float32)
        home = per_slot[s][2][...] + home + last[s].astype(jnp.float32)
        mixed[s][...] = home.astype(jnp.bfloat16)
    for copy in (copy for some in copies[1:] for copy in some):
        copy.wait()


def hidden_back(
    lengths, back_rows, grads, hidden, normed, gain, router, w_attn, experts, qkvs, bias, full, total, own_out,
    rest_out, scale, head_size,
):
    slots, count, span_rows, own_width = qkvs.shape
    model_width = hidden[0].shape[1]
    heads = bias.shape[0]
    whole = pl.BlockSpec(memory_space=pltpu.VMEM)
    f32, bf16 = jnp.float32, jnp.bfloat16
    each = [grads]
    for s in range(slots):
        each += [back_rows[s], hidden[s], normed[s]]
    each += [*own_out, *rest_out]
    own_shape = (count, span_rows, own_width // 3)
    got = pl.pallas_call(
        functools.partial(hidden_kernel, experts, scale, head_size, slots),
        grid=(1,),
        in_specs=[
            pl.BlockSpec(memory_space=pltpu.SMEM),
            whole,
            whole,
            pl.BlockSpec((model_width, model_width), lambda i: (0, 3)),
            *[pl.BlockSpec(memory_space=pl.ANY)] * 4,
        ]
        + [whole] * (len(each) - 4 * slots)
        + [pl.BlockSpec(memory_space=pl.ANY)] * (4 * slots),
        out_specs=[whole] * (5 * slots + 3),
        out_shape=[
            jax.ShapeDtypeStruct((span_rows, model_width), f32),
            jax.ShapeDtypeStruct((span_rows, model_width), bf16),
            jax.ShapeDtypeStruct((model_width, router.shape[1]), f32),
            jax.ShapeDtypeStruct((1, model_width), f32),
        ]
        * slots
        + [jax.ShapeDtypeStruct((span_rows, model_width), bf16)] * slots
        + [
            jax.ShapeDtypeStruct(qkvs.shape[1:], bf16),
            jax.ShapeDtypeStruct((heads, 1, bias.shape[2] + span_rows), f32),
            jax.ShapeDtypeStruct((slots - 1,) + own_shape, bf16),
        ],
        scratch_shapes=[
            pltpu.VMEM((slots,) + own_shape, bf16),
            pltpu.VMEM(own_shape, bf16),
            pltpu.VMEM((span_rows, model_width), bf16),
            pltpu.SemaphoreType.DMA((slots, 2, count)),
            *[pltpu.VMEM((slots, span_rows, model_width), bf16)] * 4,
            pltpu.SemaphoreType.DMA((2, 6)),
            pltpu.VMEM(qkvs.shape[1:], bf16),
            pltpu.VMEM(bias.shape, f32),
            pltpu.VMEM(full.shape[1:], f32),
            pltpu.VMEM(full.shape[1:], f32),
            pltpu.VMEM((2 * slots, span_rows, model_width), bf16),
            pltpu.SemaphoreType.DMA((8,)),
        ]
        + backward_work(count, span_rows, head_size),
        cost_estimate=cost(20e9, 20e6),
        compiler_params=remote_params(1),
        name="hidden_back",
    )(lengths, gain, router, w_attn, qkvs, bias, full, total, *each)
    return [got[4 * s : 4 * s + 4] for s in range(slots)], got[4 * slots : 5 * slots], got[5 * slots :]


def near_others(dp, ep):
    core, across = lax.rem(dp, 2), dp // 2
    return (
        {"dp": across * 2 + (1 - core)},
        {"dp": (1 - across) * 2 + core},
        {"ep": 1 - ep},
    )


def second_kernel(
    scale, head_size, slots, length_ref, former_ref, normed_all, qkv_all, bias_all, grad_ref, full_all, total_all,
    *refs,
):
    attended, proj, refs = refs[:slots], refs[slots : 2 * slots], refs[2 * slots :]
    ring_ref, line_ref, arrived_ref, early_ref, weight_ref, rows_ref = refs[:6]
    sums, low, got_core, got_x, got_y, leaving, coming, sems, near_sems, last_sems = refs[6:16]
    early_sems, held_refs, work = refs[16], refs[17:23], refs[23:]
    normed_ref, qkv_ref, bias_ref, full_ref, total_ref, load_sems = held_refs
    count = qkv_ref.shape[0]
    mine = lax.axis_index("cp")
    loads = [
        pltpu.make_async_copy(source, target, load_sems.at[at])
        for at, (source, target) in enumerate(
            (
                (qkv_all.at[1], qkv_ref),
                (bias_all, bias_ref),
                (full_all.at[1], full_ref),
                (total_all.at[1], total_ref),
                (normed_all.at[0], normed_ref),
            )
        )
    ]
    for load in loads:
        load.start()
    dp, ep = lax.axis_index("dp"), lax.axis_index("ep")
    core, across = lax.rem(dp, 2), dp // 2
    others = near_others(dp, ep)
    greet(*ring_others(mine, count), *others)
    copies = deliveries(former_ref, arrived_ref, sems, mine, count)
    for copy in copies:
        copy.start()
    arrived_ref[0] = former_ref[0]
    height = sums.shape[0] // 2
    sizes = (height, height // 2, height // 4)
    bits = (core, across, ep)
    landing = (got_core, got_x, got_y)
    total = None
    for s in range(slots):
        term = dot_tn(attended[s][...], proj[s][...])
        total = term if total is None else total + term
    sums[...] = total

    def low_part(stage):
        return low.at[stage, pl.ds(0, sizes[stage])]

    def stage_copy(stage):
        return push(
            low_part(stage), landing[stage], near_sems.at[0, stage], near_sems.at[1, stage], others[stage]
        )

    def start_of(stage):
        start = 0
        for former in range(stage):
            start = start + bits[former] * sizes[former]
        return start

    def begin(stage):
        at = start_of(stage) + (1 - bits[stage]) * sizes[stage]
        away = sums[pl.ds(pl.multiple_of(at, 128), sizes[stage]), :]
        low[stage, : sizes[stage]] = away.astype(jnp.bfloat16)
        stage_copy(stage).start()

    def finish(stage):
        stage_copy(stage).wait()
        at = pl.ds(pl.multiple_of(start_of(stage + 1), 128), sizes[stage])
        sums[at, :] = sums[at, :] + landing[stage][...].astype(jnp.float32)

    early = deliveries(ring_ref, early_ref, early_sems, mine, count, pl.ds(0, early_ref.shape[2]))

    def after_pair(pair):
        @pl.when(pair == 0)
        def _():
            for copy in early:
                copy.start()

        for stage in range(2):

            @pl.when(pair == stage)
            def _():
                finish(stage)
                begin(stage + 1)

    begin(0)
    for load in loads:
        load.wait()
    backward_body(
        mine, length_ref[1], scale, head_size, qkv_ref, bias_ref, grad_ref.at[0], full_ref, total_ref,
        ring_ref, line_ref, work, after_pair,
    )
    finish(2)
    at = pl.ds(pl.multiple_of(start_of(3), 128), sizes[2])
    groups = leaving.shape[2] // 128
    for j in range(count):
        owner = lax.rem(mine + (count - j), count)
        for group in range(groups):
            lanes = pl.ds(pl.multiple_of((group * count + owner) * 128, 128), 128)
            part = sums[at, lanes]
            leaving[j, :, group * 128 : (group + 1) * 128] = part.astype(jnp.bfloat16)
            if j == 0:
                rows_ref[:, group * 128 : (group + 1) * 128] = part
    last = deliveries(leaving, coming, last_sems, mine, count)
    for copy in last:
        copy.start()
    total = None
    for j in range(count):
        term = dot_tn(normed_ref[j], former_ref[j])
        total = term if total is None else total + term
    weight_ref[...] = total
    for copy in last:
        copy.wait()
    for j in range(1, count):
        rows_ref[...] = rows_ref[...] + coming[j].astype(jnp.float32)
    for copy in copies + early:
        copy.wait()


def second_back(
    lengths, former, normed_all, qkvs, bias, grads, full, total, attended, proj, scale, head_size, waits=()
):
    slots, count, span_rows, own_width = qkvs.shape
    model_width = normed_all.shape[3]
    whole = pl.BlockSpec(memory_space=pltpu.VMEM)
    some = pl.BlockSpec(memory_space=pl.ANY)
    f32, bf16 = jnp.float32, jnp.bfloat16
    rows_shape = (model_width // 8, own_width // 3)
    return pl.pallas_call(
        held(
            functools.partial(second_kernel, scale, head_size, slots), 8 + 2 * slots, len(waits)
        ),
        grid=(1,),
        in_specs=[
            pl.BlockSpec(memory_space=pltpu.SMEM),
            whole,
            some,
            some,
            some,
            whole,
            some,
            some,
        ]
        + [whole] * (2 * slots)
        + anywhere(waits),
        out_specs=[whole] * 6,
        out_shape=[
            jax.ShapeDtypeStruct(qkvs.shape[1:], bf16),
            jax.ShapeDtypeStruct((bias.shape[0], 1, bias.shape[2] + span_rows), f32),
            jax.ShapeDtypeStruct(qkvs.shape[1:], bf16),
            jax.ShapeDtypeStruct((count, span_rows, 384), bf16),
            jax.ShapeDtypeStruct((model_width, own_width), f32),
            jax.ShapeDtypeStruct(rows_shape, f32),
        ],
        scratch_shapes=[
            pltpu.VMEM((model_width, model_width), f32),
            pltpu.VMEM((3, model_width // 2, model_width), bf16),
            pltpu.VMEM((model_width // 2, model_width), bf16),
            pltpu.VMEM((model_width // 4, model_width), bf16),
            pltpu.VMEM((model_width // 8, model_width), bf16),
            pltpu.VMEM((count,) + rows_shape, bf16),
            pltpu.VMEM((count,) + rows_shape, bf16),
            pltpu.SemaphoreType.DMA((2, count)),
            pltpu.SemaphoreType.DMA((2, 3)),
            pltpu.SemaphoreType.DMA((2, count)),
            pltpu.SemaphoreType.DMA((2, count)),
            pltpu.VMEM(normed_all.shape[1:], bf16),
            pltpu.VMEM(qkvs.shape[1:], bf16),
            pltpu.VMEM(bias.shape, f32),
            pltpu.VMEM(full.shape[1:], f32),
            pltpu.VMEM(full.shape[1:], f32),
            pltpu.SemaphoreType.DMA((5,)),
        ]
        + backward_work(count, span_rows, head_size),
        cost_estimate=cost(20e9, 20e6),
        compiler_params=remote_params(2),
        name="second_back",
    )(lengths, former, normed_all, qkvs, bias, grads, full, total, *attended, *proj, *waits)


def token_body(mine, input_ref, hidden_ref, gain_ref, weight_ref, part_refs, own_ref, out_ref):
    count = part_refs[0].shape[0]
    model_width = input_ref.shape[1]
    total = None
    for j in range(count):
        owner = lax.rem(mine + j, count)
        pieces = []
        for group in range(own_ref.shape[2] // 384):
            for which in range(3):
                at = which * model_width + (group * count + owner) * 128
                pieces.append(weight_ref[:, pl.ds(pl.multiple_of(at, 128), 128)])
        part = own_ref[0] if j == 0 else jnp.concatenate([ref[j] for ref in part_refs], axis=1)
        term = dot_nt(part, jnp.concatenate(pieces, axis=1))
        total = term if total is None else total + term
    inputs = input_ref[...].astype(jnp.float32)
    back = norm_back(total, inputs, root_scale(inputs), gain_ref[...])
    out_ref[...] = (hidden_ref[...] + back).astype(jnp.bfloat16)


def final_kernel(
    slots, ring_ref, early_ref, normed_all, former_all, own_w_all, arrived_ref, blocks_ref, small_ref, gain_ref,
    weight_all, tokens_ref, *refs
):
    inputs = [slot_of(tokens_ref, s, slots) for s in range(slots)]
    hidden_all, refs = refs[:slots], refs[slots:]
    outs, refs = refs[:slots], refs[slots:]
    small_out, attn_out = refs[:2]
    coming, here, sum_blocks, low_blocks, small_now, small_in, sems, near_sems, small_sems = refs[2:11]
    got_core, got_x, got_y, normed_ref, former_ref, own_w_ref, weight_ref, hidden_refs, load_sems = refs[11:]
    hiddens = [hidden_refs.at[s] for s in range(slots)]
    loads = [
        pltpu.make_async_copy(source, target, load_sems.at[at])
        for at, (source, target) in enumerate(
            (
                (normed_all.at[1], normed_ref),
                (former_all, former_ref),
                (own_w_all, own_w_ref),
                (weight_all.at[:, pl.ds(0, weight_ref.shape[1])], weight_ref),
                *((hidden_all[s], hiddens[s]) for s in range(slots)),
            )
        )
    ]
    for load in loads:
        load.start()
    count = ring_ref.shape[0]
    mine = lax.axis_index("cp")
    dp, ep = lax.axis_index("dp"), lax.axis_index("ep")
    core, across = lax.rem(dp, 2), dp // 2
    core_other, x_other, y_other = near_others(dp, ep)
    greet(*ring_others(mine, count), core_other, x_other, y_other)
    late = ring_ref.shape[2] - early_ref.shape[2]
    copies = deliveries(ring_ref, coming, sems, mine, count, pl.ds(early_ref.shape[2], late))
    for copy in copies:
        copy.start()

    for load in loads[:3]:
        load.wait()
    total = former_ref[...]
    for j in range(count):
        total = total + dot_tn(normed_ref[j], ring_ref[j])
    ones = jnp.ones((8, total.shape[1]), jnp.float32)
    first_gain = lax.dot_general(
        ones,
        total * own_w_ref[...].astype(jnp.float32),
        (((1,), (1,)), ((), ())),
        precision=lax.Precision.HIGHEST,
        preferred_element_type=jnp.float32,
    )
    row = lax.broadcasted_iota(jnp.int32, small_ref.shape, 0)
    small_now[0] = jnp.where(row == 6, first_gain / gain_ref[...], small_ref[...])
    groups = total.shape[1] // 384
    for group in range(groups):
        for which in range(3):
            at = (group * 3 + which) * 128
            part = total[:, at : at + 128]
            sum_blocks[which % 2, which // 2, group] = part
            low_blocks[which % 2, which // 2, group] = part.astype(jnp.bfloat16)
        height = blocks_ref.shape[0]
        here_rows = pl.ds(pl.multiple_of((core * 4 + across * 2 + ep) * height, 128), height)
        part = blocks_ref[:, group * 128 : (group + 1) * 128]
        sum_blocks[1, 1, group] = jnp.zeros_like(sum_blocks[1, 1, group])
        low_blocks[1, 1, group] = jnp.zeros_like(low_blocks[1, 1, group])
        sum_blocks[1, 1, group, here_rows] = part
        low_blocks[1, 1, group, here_rows] = part.astype(jnp.bfloat16)
    first = push(low_blocks.at[1 - core], got_core, near_sems.at[0, 0], near_sems.at[1, 0], core_other)
    first.start()

    stages = [core_other, x_other, y_other]
    step = 1
    while step < count:
        flip = mine + step - 2 * step * lax.rem(mine // step, 2)
        stages.append({"cp": flip})
        step *= 2

    def small_push(at):
        return push(small_now.at[at], small_in.at[at], small_sems.at[0, at], small_sems.at[1, at], stages[at])

    small_push(0).start()
    for load in loads[3:]:
        load.wait()
    token_body(mine, inputs[0], hiddens[0], gain_ref, weight_ref, [arrived_ref], arrived_ref, outs[0])
    first.wait()
    here[...] = sum_blocks[core] + got_core[...].astype(jnp.float32)
    low_blocks[0, 0] = here[1 - across].astype(jnp.bfloat16)
    second = push(low_blocks.at[0, 0], got_x, near_sems.at[0, 1], near_sems.at[1, 1], x_other)
    second.start()
    for at in range(len(stages)):
        small_push(at).wait()
        now = small_now[at] + small_in[at]
        if at + 1 < len(stages):
            small_now[at + 1] = now
            small_push(at + 1).start()
        else:
            small_out[...] = now
        if at == 1:
            second.wait()
            sum_blocks[0, 0] = here[across] + got_x[...].astype(jnp.float32)
            low_blocks[0, 1, 0] = sum_blocks[0, 0, 1 - ep].astype(jnp.bfloat16)
            third = push(low_blocks.at[0, 1, 0], got_y, near_sems.at[0, 2], near_sems.at[1, 2], y_other)
            third.start()
    for copy in copies:
        copy.wait()
    token_body(mine, inputs[1], hiddens[1], gain_ref, weight_ref, [early_ref, coming], ring_ref, outs[1])
    third.wait()
    attn_out[...] = sum_blocks[0, 0, ep] + got_y[...].astype(jnp.float32)


def final_back(ring, early, normed_all, former, own_w, arrived, blocks, small, gain, w_attn, inputs, hiddens):
    count, span_rows, own_width = ring.shape
    slots = len(hiddens)
    model_width = hiddens[0].shape[1]
    groups = blocks.shape[1] // 128
    whole = pl.BlockSpec(memory_space=pltpu.VMEM)
    f32, bf16 = jnp.float32, jnp.bfloat16
    some = pl.BlockSpec(memory_space=pl.ANY)
    stages = 3 + (count - 1).bit_length()
    tile = (model_width, 128)
    return pl.pallas_call(
        functools.partial(final_kernel, slots),
        grid=(1,),
        in_specs=[
            whole,
            whole,
            some,
            some,
            some,
            whole,
            whole,
            whole,
            whole,
            some,
            whole,
        ]
        + [some] * slots,
        out_specs=[whole] * (slots + 2),
        out_shape=[jax.ShapeDtypeStruct((span_rows, model_width), bf16)] * slots
        + [jax.ShapeDtypeStruct(small.shape, f32), jax.ShapeDtypeStruct(tile, f32)],
        scratch_shapes=[
            pltpu.VMEM((count, span_rows, own_width - early.shape[2]), bf16),
            pltpu.VMEM((2, groups) + tile, f32),
            pltpu.VMEM((2, 2, groups) + tile, f32),
            pltpu.VMEM((2, 2, groups) + tile, bf16),
            pltpu.VMEM((stages,) + small.shape, f32),
            pltpu.VMEM((stages,) + small.shape, f32),
            pltpu.SemaphoreType.DMA((2, count)),
            pltpu.SemaphoreType.DMA((2, 3)),
            pltpu.SemaphoreType.DMA((2, stages)),
            pltpu.VMEM((2, groups) + tile, bf16),
            pltpu.VMEM((groups,) + tile, bf16),
            pltpu.VMEM(tile, bf16),
            pltpu.VMEM(normed_all.shape[1:], bf16),
            pltpu.VMEM(former.shape, f32),
            pltpu.VMEM(own_w.shape, bf16),
            pltpu.VMEM((model_width, 3 * model_width), bf16),
            pltpu.VMEM((slots, span_rows, model_width), f32),
            pltpu.SemaphoreType.DMA((4 + slots,)),
        ],
        cost_estimate=cost(20e9, 20e6),
        compiler_params=remote_params(3),
        name="final_back",
    )(ring, early, normed_all, former, own_w, arrived, blocks, small, gain, w_attn, inputs, *hiddens)


gelu_inner = 0.7978845608028654
gelu_cubic = 0.044715


def place_body(base, chosen_ref, pairs, outs):
    capacity = pairs[0][0].shape[0]
    span = outs[0].shape[0]
    both = [
        (mine[...].astype(jnp.float32) + theirs[...].astype(jnp.float32)).astype(jnp.bfloat16)
        for mine, theirs in pairs
    ]
    for at, out in enumerate(outs):
        total = None
        for expert in range(len(pairs)):
            ids = lax.broadcasted_iota(jnp.int32, (span, capacity), 1) + (base + expert * capacity)
            hot = jnp.zeros((span, capacity), jnp.float32)
            for choice in range(chosen_ref.shape[1]):
                chosen = chosen_ref[at * span : (at + 1) * span, choice : choice + 1]
                hot = hot + jnp.where(ids == chosen, 1.0, 0.0)
            term = dot_nn(hot.astype(jnp.bfloat16), both[expert])
            total = term if total is None else total + term
        out[...] = total.astype(jnp.bfloat16)


def return_kernel(experts, slots, target_ref, *refs):
    held_pairs = 2 * (1 + experts)
    back, far_outs, refs = refs[:held_pairs], refs[held_pairs : 2 * held_pairs], refs[2 * held_pairs :]
    backs, refs = refs[:slots], refs[slots:]
    out_own, out_rest, refs = refs[:slots], refs[slots : 4 * slots], refs[4 * slots :]
    here, got, far, last, low = refs[:5]
    outs, load_sems, sems = refs[5 : 5 + held_pairs], refs[5 + held_pairs], refs[6 + held_pairs]
    dp, ep = lax.axis_index("dp"), lax.axis_index("ep")
    _, x_other, y_other = near_others(dp, ep)
    base = ep * (experts * back[0].shape[2])
    loads = [
        pltpu.make_async_copy(source, target, load_sems.at[i])
        for i, (source, target) in enumerate(zip(far_outs, outs))
    ]
    for load in loads:
        load.start()

    def rows_of(held_refs, source):
        if source == 0:
            return [(held_refs[0].at[e, 0], held_refs[1].at[e, 0]) for e in range(experts)]
        return [
            (held_refs[2 + 2 * e].at[0, source - 1], held_refs[3 + 2 * e].at[0, source - 1])
            for e in range(experts)
        ]

    def place(held_refs, source, targets):
        place_body(base, target_ref.at[source], rows_of(held_refs, source), targets)

    firsts = [
        push(here.at[1, 0], got.at[0], sems.at[0, 0], sems.at[1, 0], x_other),
        push(here.at[2, 1], got.at[1], sems.at[0, 1], sems.at[1, 1], y_other),
        push(here.at[3, 0], far.at[0], sems.at[0, 2], sems.at[1, 2], x_other),
        push(here.at[3, 1], far.at[1], sems.at[0, 3], sems.at[1, 3], y_other),
    ]
    ends = [
        push(low.at[0], last.at[0], sems.at[0, 4], sems.at[1, 4], y_other),
        push(low.at[1], last.at[1], sems.at[0, 5], sems.at[1, 5], x_other),
    ]
    greet(x_other, y_other)
    halves = lambda source: [here.at[source, s] for s in range(slots)]
    place(back, 3, halves(3))
    firsts[2].start()
    firsts[3].start()
    place(back, 1, halves(1))
    firsts[0].start()
    place(back, 2, halves(2))
    firsts[1].start()
    place(back, 0, halves(0))
    for load in loads:
        load.wait()
    for at, (former, source) in enumerate(((2, 2), (3, 1))):
        firsts[former].wait()
        low[at] = (here[source, at].astype(jnp.float32) + far[at].astype(jnp.float32)).astype(jnp.bfloat16)
        ends[at].start()
    place(outs, 0, out_own)
    for source in range(1, 4):
        place(outs, source, out_rest[(source - 1) * slots : source * slots])
    for s in range(slots):
        firsts[s].wait()
        backs[s][...] = here[0, s].astype(jnp.float32) + got[s].astype(jnp.float32)
    for s in range(slots):
        ends[s].wait()
        backs[s][...] = backs[s][...] + last[s].astype(jnp.float32)


def return_rows(targets, backs, outs, slots, waits=()):
    experts = len(backs) // 2 - 1
    model_width = outs[0].shape[-1]
    span_rows = targets.shape[1] // slots
    wide = backs[0].shape[-1]
    whole = pl.BlockSpec(memory_space=pltpu.VMEM)
    f32, bf16 = jnp.float32, jnp.bfloat16
    half = pltpu.VMEM((slots, span_rows, wide), bf16)
    got = pl.pallas_call(
        held(
            functools.partial(return_kernel, experts, slots),
            1 + len(backs) + len(outs),
            len(waits),
        ),
        in_specs=[whole] + [whole] * len(backs) + anywhere(outs) + anywhere(waits),
        out_specs=[whole] * (5 * slots),
        out_shape=[
            *[jax.ShapeDtypeStruct((span_rows, wide), f32)] * slots,
            *[jax.ShapeDtypeStruct((span_rows, model_width), bf16)] * (4 * slots),
        ],
        scratch_shapes=[pltpu.VMEM((4, slots, span_rows, wide), bf16), half, half, half, half]
        + [pltpu.VMEM(a.shape, bf16) for a in outs]
        + [pltpu.SemaphoreType.DMA((len(outs),)), pltpu.SemaphoreType.DMA((2, 6))],
        cost_estimate=cost(20e9, 20e6),
        compiler_params=remote_params(4),
        name="return_rows",
    )(targets, *backs, *outs, *waits)
    return got[:slots], got[slots : 2 * slots], got[2 * slots :]


def expert_body(experts, own_units, expert, skip, given, refs, weights, router_ref):
    back_mine, back_theirs, out_mine, out_theirs, kept_rows, kept_units = refs
    gate_ref, up_ref, down_ref = weights
    capacity, model_width = given[0].shape[2:]
    rows = jnp.concatenate([given[0][0, 0], given[1][0, 0]], axis=0)
    grads = jnp.concatenate([given[2][0, 0], given[3][0, 0]], axis=0)
    kept_rows[0, 0, 0] = rows
    kept_rows[1, 0, 0] = grads
    lane = lax.broadcasted_iota(jnp.int32, (1, router_ref.shape[1]), 1)
    probs = router_of(rows, router_ref[...], experts)
    gates = jnp.sum(jnp.where(lane == expert, probs, 0.0), axis=1, keepdims=True)
    unit = lax.broadcasted_iota(jnp.int32, (1, gate_ref.shape[2]), 1) - skip
    own = jnp.logical_and(unit >= 0, unit < own_units)
    gate_w, up_w, down_w = gate_ref[0], up_ref[0], down_ref[0]
    gate_pre = dot_nn(rows, gate_w)
    up_pre = jnp.where(own, dot_nn(rows, up_w), 0.0)
    square = gate_pre * gate_pre
    tanh = jnp.tanh(gelu_inner * gate_pre * (1.0 + gelu_cubic * square))
    half = 0.5 + 0.5 * tanh
    active = gate_pre * half
    slope = half + active * (1.0 - tanh) * (gelu_inner * (1.0 + 3.0 * gelu_cubic * square))
    inner = active * up_pre
    low_inner = inner.astype(jnp.bfloat16)
    plain_grads = jnp.where(own, dot_nn(grads, down_w), 0.0)
    gate_grads = jnp.sum(plain_grads * low_inner.astype(jnp.float32), axis=1, keepdims=True)
    inner_grads = plain_grads * gates
    low_gate = (inner_grads * up_pre * slope).astype(jnp.bfloat16)
    low_up = (inner_grads * active).astype(jnp.bfloat16)
    kept_units[0, 0, 0] = low_gate
    kept_units[1, 0, 0] = low_up
    kept_units[2, 0, 0] = (inner * gates).astype(jnp.bfloat16)
    back = (dot_nt(low_gate, gate_w) + dot_nt(low_up, up_w)).astype(jnp.bfloat16)
    shares = jnp.where(lane == expert, gate_grads, 0.0).astype(jnp.bfloat16)
    out = (gates * dot_nt(low_inner, down_w)).astype(jnp.bfloat16)
    for at, back_ref, out_ref in ((0, back_mine, out_mine), (1, back_theirs, out_theirs)):
        part = slice(at * capacity, (at + 1) * capacity)
        back_ref[0, 0, :, :model_width] = back[part]
        back_ref[0, 0, :, model_width:] = shares[part]
        out_ref[0, 0] = out[part]


def expert_kernel(experts, own_units, kept_count, first_ref, window_ref, *refs):
    given, refs = refs[:4], refs[4:]
    router_ref, weights, refs = refs[0], refs[1:4], refs[4 + kept_count :]
    expert = first_ref[0] + pl.program_id(0)
    expert_body(experts, own_units, expert, window_ref[1], given, refs, weights, router_ref)


def own_kernel(experts, own_units, *refs):
    given, router_ref, weights, refs = refs[:4], refs[4], refs[5:8], refs[8:]
    target_ref, over_ref, up_ref, normed_ref, refs = refs[0], refs[1], refs[2], refs[3], refs[4:]
    results, kept, (mine_ref, theirs_ref), refs = refs[:4], refs[4:6], refs[6:8], refs[8:]
    coming, picked, held_w, held_rows, held_units = refs[:5]
    sems, core_sems, home_sems, load_sems, keep_sems = refs[5:]
    exp_dev, capacity = picked.shape[1:3]
    dp, ep = lax.axis_index("dp"), lax.axis_index("ep")
    core_other, x_other, y_other = near_others(dp, ep)
    skip = lax.rem(dp * own_units, 128)

    def copy(at):
        source, other = (
            (normed_ref, x_other),
            (normed_ref, y_other),
            (over_ref, y_other),
            (coming.at[1], x_other),
        )[at]
        return push(source, coming.at[at], sems.at[0, at], sems.at[1, at], other)

    def load(expert, which):
        lanes = pl.ds(pl.multiple_of(dp * own_units - skip, 128), held_w.shape[4])
        return pltpu.make_async_copy(
            weights[which].at[pl.ds(expert, 1), :, lanes],
            held_w.at[expert, which],
            load_sems.at[expert, which],
        )

    def keep(expert, kind):
        held_ref = (held_rows, held_units)[kind]
        return pltpu.make_async_copy(
            held_ref.at[expert, :, 0, 0], kept[kind].at[:, expert, 0], keep_sems.at[expert, kind]
        )

    for expert in range(exp_dev):
        for which in range(3):
            load(expert, which).start()
    greet(core_other, x_other, y_other)
    for at in range(3):
        copy(at).start()
    for expert in range(exp_dev):
        if expert == 1:
            copy(1).wait_recv()
            copy(3).start()
        for which in range(3):
            load(expert, which).wait()
        here = pl.ds(expert, 1)
        expert_body(
            experts,
            own_units,
            ep * exp_dev + expert,
            skip,
            [part.at[:, here] for part in given],
            [part.at[here] for part in results] + [held_rows.at[expert], held_units.at[expert]],
            [held_w.at[expert, which] for which in range(3)],
            router_ref,
        )
        for kind in range(2):
            keep(expert, kind).start()

    base = ep * (exp_dev * capacity)
    blocks = (
        (over_ref, coming.at[0]),
        (up_ref, coming.at[1]),
        (coming.at[2], coming.at[3]),
    )

    def across_cores(k):
        return push(picked.at[k], theirs_ref.at[k], core_sems.at[0, k], core_sems.at[1, k], core_other)

    def home(k):
        return pltpu.make_async_copy(picked.at[k], mine_ref.at[k], home_sems.at[k])

    for k, waits in enumerate(((0,), (), (2, 3))):
        for at in waits:
            copy(at).wait_recv()
        chosen = [target_ref.at[k + 1, s] for s in range(target_ref.shape[1])]
        pick_body(base, capacity, exp_dev, chosen, blocks[k], picked.at[k])
        across_cores(k).start()
        home(k).start()
    for at in range(4):
        copy(at).wait_send()
    for k in range(3):
        across_cores(k).wait()
        home(k).wait()
    for expert in range(exp_dev):
        for kind in range(2):
            keep(expert, kind).wait()


def own_experts(given, router, weights, target, over, up, normed, total, experts, units):
    _, exp_dev, capacity, model_width = given[0].shape
    span_rows = normed.shape[0]
    wide_units = aligned_units(units)
    tile = 2 * capacity
    bf16 = jnp.bfloat16
    shape = jax.ShapeDtypeStruct
    picked = (3, exp_dev, capacity, model_width)
    wide = model_width + 128
    keeps = ((2, model_width), (3, wide_units))
    whole = pl.BlockSpec(memory_space=pltpu.VMEM)
    some = pl.BlockSpec(memory_space=pl.ANY)
    got = pl.pallas_call(
        functools.partial(own_kernel, experts, units),
        grid=(1,),
        in_specs=[whole] * 5 + [some] * 3 + [whole] * 4,
        out_specs=[whole] * 4 + [some] * 4,
        out_shape=[shape((exp_dev, 1, capacity, wide), bf16)] * 2
        + [shape((exp_dev, 1, capacity, model_width), bf16)] * 2
        + [shape((kinds, exp_dev, total, tile, width), bf16) for kinds, width in keeps]
        + [shape(picked, bf16)] * 2,
        scratch_shapes=[
            pltpu.VMEM((4, span_rows, model_width), bf16),
            pltpu.VMEM(picked, bf16),
            pltpu.VMEM((exp_dev, 3, 1, model_width, wide_units), bf16),
        ]
        + [pltpu.VMEM((exp_dev, kinds, 1, 1, tile, width), bf16) for kinds, width in keeps]
        + [
            pltpu.SemaphoreType.DMA((2, 4)),
            pltpu.SemaphoreType.DMA((2, 3)),
            pltpu.SemaphoreType.DMA((3,)),
            pltpu.SemaphoreType.DMA((exp_dev, 3)),
            pltpu.SemaphoreType.DMA((exp_dev, 2)),
        ],
        cost_estimate=cost(20e9, 16e6),
        compiler_params=remote_params(5),
        name="own_experts",
    )(*given, router, *weights, target, over, up, normed)
    return got[:4], got[4:6], got[6:]


def run_experts(first, window, given, router, weights, kept, at, total, experts, units, chosen):
    low, high = chosen
    sources, exp_dev, capacity, model_width = given[0].shape
    wide_units = aligned_units(units)
    tile = 2 * capacity

    given_rows = pl.BlockSpec(
        (1, 1, capacity, model_width), lambda e, k, f, w: (k, low + e, 0, 0)
    )
    out = lambda width: pl.BlockSpec((1, 1, capacity, width), lambda e, k, f, w: (e, k, 0, 0))
    wide, rows = out(model_width + 128), out(model_width)
    weight = pl.BlockSpec(
        (pl.Element(1), pl.Element(model_width), pl.Element(wide_units)),
        lambda e, k, f, w: (low + e, 0, pl.multiple_of(w[0], 128)),
    )
    keep = lambda kinds, width: pl.BlockSpec(
        (kinds, 1, 1, tile, width), lambda e, k, f, w: (0, low + e, at + k, 0, 0)
    )
    keeps = ((2, model_width), (3, wide_units))
    kept = list(kept)
    out_of = lambda width: jax.ShapeDtypeStruct(
        (high - low, sources, capacity, width), jnp.bfloat16
    )
    back_shape, out_shape = out_of(model_width + 128), out_of(model_width)
    got = pl.pallas_call(
        functools.partial(expert_kernel, experts, units, len(kept)),
        grid_spec=pltpu.PrefetchScalarGridSpec(
            num_scalar_prefetch=2,
            grid=(high - low, sources),
            in_specs=[given_rows] * 4
            + [
                pl.BlockSpec(router.shape, lambda e, k, f, w: (0, 0)),
                weight,
                weight,
                weight,
            ]
            + anywhere(kept),
            out_specs=[wide, wide, rows, rows] + [keep(*kinds) for kinds in keeps],
        ),
        out_shape=[back_shape, back_shape, out_shape, out_shape]
        + [
            jax.ShapeDtypeStruct((kinds, exp_dev, total, tile, width), jnp.bfloat16)
            for kinds, width in keeps
        ],
        input_output_aliases={10 + i: 4 + i for i in range(len(kept))},
        cost_estimate=cost(20e9 * sources, 8e6 * sources),
        compiler_params=compiler_params(),
        name="expert_rows",
    )(first + low, window, *given, router, *weights, *kept)
    return got[:4], got[4:]


def aligned_units(units):
    return (units + 127) // 128 * 128


def weight_kernel(window_ref, rows_ref, units_ref, weight_ref, total):
    pieces, _, piece, model_width = weight_ref.shape
    units = units_ref[0, 0].reshape(-1, units_ref.shape[-1])
    total[...] = dot_tn(units, rows_ref[0, 0].reshape(-1, model_width))
    skip = pl.multiple_of(window_ref[1], 64)
    for at in range(pieces):
        weight_ref[at, 0] = total[pl.ds(skip + at * piece, piece), :].astype(jnp.bfloat16)


def weight_grads(window, kept, expert, pieces, units, waits=()):
    kept_rows, kept_units = kept
    tiles, tile, model_width = kept_rows.shape[2:]
    wide_units = kept_units.shape[4]
    shape = (pieces, 3, units // pieces, model_width)
    return pl.pallas_call(
        held(weight_kernel, 3, len(waits)),
        grid=(3,),
        in_specs=[
            pl.BlockSpec(memory_space=pltpu.SMEM),
            pl.BlockSpec((1, 1, tiles, tile, model_width), lambda i: (i // 2, expert, 0, 0, 0)),
            pl.BlockSpec((1, 1, tiles, tile, wide_units), lambda i: (i, expert, 0, 0, 0)),
        ]
        + anywhere(waits),
        out_specs=pl.BlockSpec((pieces, 1) + shape[2:], lambda i: (0, i, 0, 0)),
        out_shape=jax.ShapeDtypeStruct(shape, jnp.bfloat16),
        scratch_shapes=[pltpu.VMEM((wide_units, model_width), jnp.float32)],
        cost_estimate=cost(20e9, 20e6),
        compiler_params=compiler_params(),
        name="weight_grads",
    )(window, kept_rows, kept_units, *waits)


def send(values, axis, pairs):
    return lax.ppermute(values, axis, pairs)


def after(values, *earlier):
    return lax.optimization_barrier((values, earlier))[0]


def fast_device(
    tokens,
    lengths,
    expert_ids,
    places,
    buckets,
    w_attn,
    bias_table,
    norm1_gain,
    norm2_gain,
    w_router,
    w_gate,
    w_up,
    w_down,
    cotangent,
):
    span_rows, slots, model_width = tokens.shape
    head_count, bucket_count = bias_table.shape
    head_size = model_width // head_count
    scale = head_size ** (-0.5)
    n_dp = lax.axis_size("dp")
    n_ep = lax.axis_size("ep")
    n_cp = lax.axis_size("cp")
    my_dp, my_ep, my_cp = (lax.axis_index(name) for name in ("dp", "ep", "cp"))
    seq_len = span_rows * n_cp
    rows = span_rows * slots
    top_count = expert_ids.shape[2]
    experts = w_router.shape[1]
    exp_dev = w_gate.shape[0]
    units = w_gate.shape[2] // n_dp
    capacity = (5 * rows * top_count + 4 * experts - 1) // (4 * experts)
    groups = model_width // (128 * n_cp)
    own_width = 3 * groups * 128
    heads_own = head_count // n_cp
    over_core = [(i, i ^ 1) for i in range(n_dp)]
    over_x = [(i, i ^ 2) for i in range(n_dp)]
    over_y = [(i, i ^ 1) for i in range(n_ep)]
    ring = [(i, (i + 1) % n_cp) for i in range(n_cp)]
    f32, bf16 = jnp.float32, jnp.bfloat16
    exact = lax.Precision.HIGHEST
    each = range(slots)

    low_in = tokens.reshape(span_rows, slots * model_width)
    low_out = cotangent.reshape(span_rows, slots * model_width)
    gain_first, gain_second = norm1_gain[None, :], norm2_gain[None, :]

    per_group = 128 // head_size
    own_heads = (
        jnp.arange(groups)[:, None] * (n_cp * per_group)
        + my_cp * per_group
        + jnp.arange(per_group)[None, :]
    ).reshape(heads_own)
    head_hot = (own_heads[:, None] == jnp.arange(head_count)[None, :]).astype(f32)
    own_table = jnp.dot(head_hot, bias_table, precision=exact)
    far_hot = (buckets[::-1][:, None] == jnp.arange(bucket_count)[None, :]).astype(f32)
    lines = jnp.einsum("hb,db->hd", own_table, far_hot, precision=exact)
    lines = jnp.concatenate([lines, jnp.full((heads_own, span_rows), minus_big, f32)], axis=1)
    target = jnp.where(places >= 0, expert_ids * capacity + places, -1)
    target = target.transpose(1, 2, 0).astype(jnp.int32)
    (
        (normed_all, qkvs, bias, full, total, w_own, target_all, over_first, up_first),
        (grads_own, grads_rest_rows, picked_own),
        fronts,
    ) = front(
        lengths,
        gain_first,
        gain_second,
        lines[:, None, :],
        target,
        w_attn,
        low_in,
        low_out,
        slots,
        n_cp,
        exp_dev,
        capacity,
        scale,
        head_size,
    )
    attended, hidden, normed_second = zip(*fronts)

    sources = target_all.shape[0]
    target_rows = target_all.transpose(0, 2, 1, 3).reshape(sources, top_count, rows)
    target_columns = target_rows.transpose(0, 2, 1)
    window_at = my_dp * units // 128 * 128
    window = jnp.stack([window_at, my_dp * units - window_at]).astype(jnp.int32)
    router_wide = jnp.concatenate(
        [w_router, jnp.zeros((model_width, 128 - experts), w_router.dtype)], axis=1
    )

    first = (my_ep * exp_dev).astype(jnp.int32).reshape(1)
    own, kept, picked_rest = own_experts(
        (*picked_own, *grads_own),
        router_wide,
        (w_gate, w_up, w_down),
        target_all,
        over_first,
        up_first,
        normed_second[1],
        sources,
        experts,
        units,
    )

    def with_theirs(mine, theirs):
        return [mine, send(theirs, "dp", over_core)]

    backs, outs = with_theirs(own[0], own[1]), with_theirs(own[2], own[3])
    weight_sums = []
    for e in range(exp_dev):
        rest, kept = run_experts(
            first,
            window,
            (*picked_rest, *grads_rest_rows),
            router_wide,
            (w_gate, w_up, w_down),
            kept,
            1,
            sources,
            experts,
            units,
            (e, e + 1),
        )
        weight_part = weight_grads(window, kept, e, n_cp, units, backs[-1:] + outs[-1:])
        backs += with_theirs(rest[0], rest[1])
        outs += with_theirs(rest[2], rest[3])
        weight_sums.append(lax.psum_scatter(weight_part, "cp", scatter_dimension=0, tiled=False))
        kept = after(kept, weight_part)
    back_rows, out_own, out_rest = return_rows(target_columns, backs, outs, slots, [weight_part])
    got, mixed, (ringed, line_first, grads_rest) = hidden_back(
        lengths,
        back_rows,
        low_out,
        hidden,
        normed_second,
        gain_second,
        router_wide,
        w_attn,
        experts,
        qkvs,
        bias,
        full,
        total,
        out_own,
        out_rest,
        scale,
        head_size,
    )
    hidden_grads, proj_grads, router_parts, gain_parts = zip(*got)
    router_grad = sum(router_parts)[:, :experts].T
    ring_second, line_second, arrived, early, weight_first, out_grad = second_back(
        lengths,
        ringed,
        normed_all,
        qkvs,
        bias,
        grads_rest,
        full,
        total,
        attended,
        proj_grads,
        scale,
        head_size,
        weight_sums[:1],
    )
    distance_grads = (line_first + line_second)[:, 0, :seq_len]
    table_grad = jnp.dot(distance_grads, far_hot, precision=exact)
    table_grad = jnp.einsum("hg,hb->gb", head_hot, table_grad, precision=exact)
    table_row = jnp.pad(table_grad.reshape(1, -1), ((0, 0), (0, model_width - table_grad.size)))
    small = jnp.concatenate(
        [router_grad, sum(gain_parts), table_row, jnp.zeros((2, model_width), f32)], axis=0
    )
    *tokens_grad, small_sum, attn_sum = final_back(
        ring_second,
        early,
        normed_all,
        weight_first,
        w_own,
        arrived,
        out_grad,
        small,
        gain_first,
        w_attn,
        low_in,
        hidden_grads,
    )
    router_sum, gain_second_sum = small_sum[:experts], small_sum[experts]
    table_sum = small_sum[experts + 1, : table_grad.size].reshape(table_grad.shape)
    gain_first_sum = small_sum[experts + 2]

    gate_sum, up_sum, down_sum = (
        jnp.stack([part[which].T.astype(f32) for part in weight_sums]) for which in range(3)
    )
    return (
        jnp.stack(mixed, axis=1),
        jnp.stack(tokens_grad, axis=1),
        attn_sum,
        table_sum,
        gain_first_sum,
        gain_second_sum,
        router_sum.T,
        gate_sum,
        up_sum,
        down_sum,
    )


def solution(mesh):
    placed = (
        P("cp", ("dp", "ep"), None),
        P(("dp", "ep")),
        P("cp", ("dp", "ep"), None),
        P("cp", ("dp", "ep"), None),
        P(),
        P(),
        P(),
        P(),
        P(),
        P(),
        P("ep", None, None),
        P("ep", None, None),
        P("ep", None, None),
        P("cp", ("dp", "ep"), None),
    )
    sizes = dict(mesh.shape)
    square = sizes["dp"] == 4 and sizes["ep"] == 2 and sizes["cp"] == 4
    return jax.shard_map(
        fast_device if square else on_device,
        mesh=mesh,
        in_specs=placed,
        out_specs=(
            P("cp", ("dp", "ep"), None),
            P("cp", ("dp", "ep"), None),
            P(None, ("dp", "ep", "cp")),
            P(),
            P(),
            P(),
            P(),
            P("ep", None, ("dp", "cp")),
            P("ep", None, ("dp", "cp")),
            P("ep", None, ("dp", "cp")),
        ),
        check_vma=False,
    )
```

profile of v0, /device:TPU:0, one launch (start us, length us, event | category | flops | bytes accessed | tf_op | source)
XLA Modules:
  0.0 519.3 jit_solution(17508239397390432930)
XLA Ops:
  7.2 0.0 copy-start
  7.2 0.0 reduce-scatter.3.cloned.1.call-start
  7.3 0.1 iota_add_fusion
  7.3 0.1 add.62
  7.4 0.8 rev.3
  8.3 0.2 fusion.11
  8.5 0.5 fusion.1
  8.9 0.6 broadcast_in_dim.25.line_ref
  9.6 2.5 copy.35
  12.1 1.2 copy.36
  13.3 0.2 copy.28
  13.6 0.6 fusion.9.target_ref
  14.2 0.8 concatenate.9.refs_4_.router_ref
  14.9 114.7 %front.1 = (bf16[2,4,256,1024]{3,2,1,0:T(8,128)(2,1)}, bf16[2,4,256,768]{3,2,1,0:T(8,128)(2,1)}, f32[4,256,1024]{2,1,0:T(8,128)}, f32[2,4,256,256]{3,2,1,0:T(8,1...) custom-call(s32[2]{0:T(128)} %refs_0_.1, ...), custom_call_target="tpu_custom_call" | custom-call | flops 3000000000 | bytes 1000000 | tf_op jit(solution)/shard_map/front/pallas_call | solution.py:852
  129.6 35.5 %own_experts.1 = (bf16[2,1,320,1152]{3,2,1,0:T(8,128)(2,1)}, bf16[2,1,320,1152]{3,2,1,0:T(8,128)(2,1)}, bf16[2,1,320,1024]{3,2,1,0:T(8,128)(2,1)}, bf16[2,1,320,...) custom-call(bf16[1,2,320,1024]{3,2,1,0:T(8,128)(2,1)} %get-tuple-ele, ...), custom_call_target="tpu_custom_call" | custom-call | flops 1000000000 | bytes 800000 | tf_op jit(solution)/shard_map/own_experts/pallas_call | solution.py:1732
  165.2 0.4 collective-permute-start
  165.6 0.1 collective-permute-start.2
  165.7 0.6 pad_add_fusion.window_ref.refs_0_
  166.3 28.3 %expert_rows.2 = (bf16[1,3,320,1152]{3,2,1,0:T(8,128)(2,1)}, bf16[1,3,320,1152]{3,2,1,0:T(8,128)(2,1)}, bf16[1,3,320,1024]{3,2,1,0:T(8,128)(2,1)}, bf16[1,3,320,...) custom-call(s32[1]{0:T(128)} %bitcast.6.first_ref, ...), custom_call_target="tpu_custom_call", output_to_operand_aliasing={{4}: (10, {}), {5}: (11, {})} | custom-call | flops 3000000000 | bytes 1200000 | tf_op jit(solution)/shard_map/expert_rows/pallas_call | solution.py:1785
  194.7 0.0 collective-permute-done.2.refs_4_.refs_8_
  194.7 0.0 copy-start.4
  194.7 1.0 copy-done.4
  195.7 0.5 copy-done.3
  196.2 18.3 %weight_grads.2 = bf16[4,3,176,1024]{3,2,1,0:T(8,128)(2,1)} custom-call(s32[2]{0:T(128)} %pad_add_fusion.window_ref.refs_0_, bf16[2,2,4,640,1024]{4,3,2,1,0:T(8,128)(2,1)} %get-tuple-element.111.refs_1_.refs_8_, bf16[3,2,4,640,768]{4,3,2,1,0:T(8,128)(2,1)} %get-tuple-element.112.refs_2_.refs_9_, bf16[2,1,320,1152]{3,2,1,0:T(8,128)(2,1)} %copy-done.3, ...), custom_call_target="tpu_custom_call" | custom-call | flops 1000000000 | bytes 1000000 | tf_op jit(solution)/shard_map/weight_grads/pallas_call | solution.py:1831
  214.5 0.0 reduce-scatter.3.cloned.1.call-update
  214.6 0.0 reduce-scatter.5.cloned.1.call-start
  214.6 0.4 collective-permute-start.1
  215.0 0.1 collective-permute-start.4
  215.2 29.1 %expert_rows.3 = (bf16[1,3,320,1152]{3,2,1,0:T(8,128)(2,1)}, bf16[1,3,320,1152]{3,2,1,0:T(8,128)(2,1)}, bf16[1,3,320,1024]{3,2,1,0:T(8,128)(2,1)}, bf16[1,3,320,...) custom-call(s32[1]{0:T(128)S(6)} %add.64.first_ref, ...), custom_call_target="tpu_custom_call", output_to_operand_aliasing={{4}: (10, {}), {5}: (11, {})} | custom-call | flops 3000000000 | bytes 1200000 | tf_op jit(solution)/shard_map/expert_rows/pallas_call | solution.py:1785
  244.3 1.4 copy-done.2
  245.7 18.5 %weight_grads.3.refs_13_ = bf16[4,3,176,1024]{3,2,1,0:T(8,128)(2,1)} custom-call(s32[2]{0:T(128)} %pad_add_fusion.window_ref.refs_0_, bf16[2,2,4,640,1024]{4,3,2,1,0:T(8,128)(2,1)} %get-tuple-element.120.refs_1_, bf16[3,2,4,640,768]{4,3,2,1,0:T(8,128)(2,1)} %get-tuple-element.121.refs_2_, bf16[1,3,320,1152]{3,2,1,0:T(8,128)(2,1)} %copy-done.2, ...), custom_call_target="tpu_custom_call" | custom-call | flops 1000000000 | bytes 1000000 | tf_op jit(solution)/shard_map/weight_grads/pallas_call | solution.py:1831
  264.3 0.0 reduce-scatter.5.cloned.1.call-update
  264.3 0.4 collective-permute-start.3
  264.8 0.1 collective-permute-start.5
  264.9 0.1 copy-done.11
  265.0 1.3 copy.29
  266.3 0.1 pad.18.clone
  266.4 5.4 %collective-permute-done.5.refs_12_ = bf16[1,3,320,1024]{3,2,1,0:T(8,128)(2,1)} collective-permute-done((bf16[1,3,320,1024]{3,2,1,0:T(8,128)(2,1)}, bf16[1,3,320,1024]{3,2,1,0:T(8,128)(2,1)}, u32[]{:S(2)}, u32[]{:S(2)}) %collective-permute-start.5) | collective-permute-done | bytes 1966112 | tf_op jit(solution)/shard_map/ppermute | solution.py:1850
  271.9 1.3 copy-done.6
  273.2 50.2 %return_rows.1 = (f32[256,1152]{1,0:T(8,128)}, f32[256,1152]{1,0:T(8,128)}, bf16[256,1024]{1,0:T(8,128)(2,1)}, bf16[256,1024]{1,0:T(8,128)(2,1)}, bf16[256,1024]...) custom-call(s32[4,512,2]{2,1,0:T(8,128)} %bitcast.73, ...), custom_call_target="tpu_custom_call" | custom-call | flops 1000000000 | bytes 1000000 | tf_op jit(solution)/shard_map/return_rows/pallas_call | solution.py:1560
  323.4 64.7 %hidden_back.1 = (f32[256,1024]{1,0:T(8,128)}, bf16[256,1024]{1,0:T(8,128)(2,1)}, f32[1024,128]{1,0:T(8,128)}, f32[1,1024]{1,0:T(1,128)}, f32[256,1024]{1,0:T(8,...) custom-call(s32[2]{0:T(128)} %refs_0_.1, ...), custom_call_target="tpu_custom_call" | custom-call | flops 1000000000 | bytes 1000000 | tf_op jit(solution)/shard_map/hidden_back/pallas_call | solution.py:1045
  388.1 1.3 copy.30
  389.4 1.2 copy.31
  390.7 0.1 pad_maximum_fusion
  390.8 2.0 copy.32
  392.9 0.0 reduce-scatter.3.cloned.1.call-done
  392.9 65.0 %second_back.1 = (bf16[4,256,768]{2,1,0:T(8,128)(2,1)}, f32[4,1,1280]{2,1,0:T(1,128)}, bf16[4,256,768]{2,1,0:T(8,128)(2,1)}, bf16[4,256,384]{2,1,0:T(8,128)(2,1)...) custom-call(s32[2]{0:T(128)} %refs_0_.1, bf16[4,256,768]{2,1,0:T(8,128)(2,1)} %get-tuple-element.137.refs_1_, ...), custom_call_target="tpu_custom_call" | custom-call | flops 1000000000 | bytes 1000000 | tf_op jit(solution)/shard_map/second_back/pallas_call | solution.py:1228
  457.9 0.7 slice_add_fusion
  458.7 0.4 fusion
  459.1 0.3 fusion.10
  459.3 0.1 reshape.85
  459.4 0.7 fusion.4.small_ref
  460.1 41.6 %final_back.1 = (bf16[256,1024]{1,0:T(8,128)(2,1)}, bf16[256,1024]{1,0:T(8,128)(2,1)}, f32[8,1024]{1,0:T(8,128)}, f32[1024,128]{1,0:T(8,128)}) custom-call(bf16[4,256,768]{2,1,0:T(8,128)(2,1)} %get-tuple-element.144.ring_ref, bf16[4,256,384]{2,1,0:T(8,128)(2,1)} %get-tuple-element.145.early_ref, ...), custom_call_target="tpu_custom_call" | custom-call | flops 1000000000 | bytes 1000000 | tf_op jit(solution)/shard_map/final_back/pallas_call | solution.py:1417
  501.8 1.4 pad_maximum_fusion.1
  503.2 2.0 copy.33
  505.2 0.7 reshape_squeeze.3
  505.9 0.6 fusion.14
  506.5 0.6 slice_bitcast_fusion.6
  507.1 0.1 slice_bitcast_fusion.1
  507.2 0.0 reduce-scatter.5.cloned.1.call-done
  507.2 1.3 slice_bitcast_fusion
  508.5 1.2 maximum_convert_fusion.2
  509.7 1.8 maximum_convert_fusion
  511.5 0.8 copy.46
  (41 shorter events, 0.1 us)
Async XLA Ops:
  7.2 1.1 copy-start
  7.2 4.9 copy-start.7
  7.2 385.7 %reduce-scatter.3.cloned.1.call-start = ((), (), s32[]{:S(2)}) async-start(), calls=%async_computation.2 | async-start | bytes 5406720 | tf_op jit(solution)/shard_map/reduce_scatter | solution.py:1983
  9.6 3.8 copy-start.14
  9.6 4.0 copy-start.15
  9.6 4.0 copy-start.16
  165.2 29.5 %collective-permute-start = (bf16[2,1,320,1152]{3,2,1,0:T(8,128)(2,1)}, bf16[2,1,320,1152]{3,2,1,0:T(8,128)(2,1)S(1)}, u32[]{:S(2)}, u32[]{:S(2)}) collective-permute-start(bf16[2,1,320,1152]{3,2,1,0:T(8,128)(2,1)} %get-tuple-element.99), channel_id=1, source_target_pairs={{0,8},{8,0},{16,24},{24,16},{1,9},{9,1},{17,25},{25,17},{2,10},{10... | collective-permute-start | bytes 4423688 | tf_op jit(solution)/shard_map/ppermute | solution.py:1850
  165.6 29.1 %collective-permute-start.2 = (bf16[2,1,320,1024]{3,2,1,0:T(8,128)(2,1)}, bf16[2,1,320,1024]{3,2,1,0:T(8,128)(2,1)S(1)}, u32[]{:S(2)}, u32[]{:S(2)}) collective-permute-start(bf16[2,1,320,1024]{3,2,1,0:T(8,128)(2,1)} %get-tuple-element.110), channel_id=1, source_target_pairs={{0,8},{8,0},{16,24},{24,16},{1,9},{9,1},{17,25},{25,17},{2,10},{10... | collective-permute-start | bytes 3932168 | tf_op jit(solution)/shard_map/ppermute | solution.py:1850
  194.7 1.1 copy-start.4
  194.7 1.5 copy-start.3
  214.6 292.7 %reduce-scatter.5.cloned.1.call-start = ((), (), s32[]{:S(2)}) async-start(), calls=%async_computation.3 | async-start | bytes 5406720 | tf_op jit(solution)/shard_map/reduce_scatter | solution.py:1983
  214.6 29.7 %collective-permute-start.1 = (bf16[1,3,320,1152]{3,2,1,0:T(8,128)(2,1)}, bf16[1,3,320,1152]{3,2,1,0:T(8,128)(2,1)S(1)}, u32[]{:S(2)}, u32[]{:S(2)}) collective-permute-start(bf16[1,3,320,1152]{3,2,1,0:T(8,128)(2,1)} %get-tuple-element.107), channel_id=1, source_target_pairs={{0,8},{8,0},{16,24},{24,16},{1,9},{9,1},{17,25},{25,17},{2,10},{10... | collective-permute-start | bytes 6635528 | tf_op jit(solution)/shard_map/ppermute | solution.py:1850
  215.0 29.3 %collective-permute-start.4 = (bf16[1,3,320,1024]{3,2,1,0:T(8,128)(2,1)}, bf16[1,3,320,1024]{3,2,1,0:T(8,128)(2,1)}, u32[]{:S(2)}, u32[]{:S(2)}) collective-permute-start(bf16[1,3,320,1024]{3,2,1,0:T(8,128)(2,1)} %get-tuple-element.117), channel_id=1, source_target_pairs={{0,8},{8,0},{16,24},{24,16},{1,9},{9,1},{17,25},{25,17},{2,10},{10... | collective-permute-start | bytes 5898248 | tf_op jit(solution)/shard_map/ppermute | solution.py:1850
  244.3 1.4 copy-start.2
  264.3 0.7 copy-start.11
  264.3 7.5 %collective-permute-start.3 = (bf16[1,3,320,1152]{3,2,1,0:T(8,128)(2,1)}, bf16[1,3,320,1152]{3,2,1,0:T(8,128)(2,1)S(1)}, u32[]{:S(2)}, u32[]{:S(2)}) collective-permute-start(bf16[1,3,320,1152]{3,2,1,0:T(8,128)(2,1)} %get-tuple-element.114), channel_id=1, source_target_pairs={{0,8},{8,0},{16,24},{24,16},{1,9},{9,1},{17,25},{25,17},{2,10},{10... | collective-permute-start | bytes 6635528 | tf_op jit(solution)/shard_map/ppermute | solution.py:1850
  264.8 7.1 %collective-permute-start.5 = (bf16[1,3,320,1024]{3,2,1,0:T(8,128)(2,1)}, bf16[1,3,320,1024]{3,2,1,0:T(8,128)(2,1)}, u32[]{:S(2)}, u32[]{:S(2)}) collective-permute-start(bf16[1,3,320,1024]{3,2,1,0:T(8,128)(2,1)} %get-tuple-element.119), channel_id=1, source_target_pairs={{0,8},{8,0},{16,24},{24,16},{1,9},{9,1},{17,25},{25,17},{2,10},{10... | collective-permute-start | bytes 5898248 | tf_op jit(solution)/shard_map/ppermute | solution.py:1850
  271.9 1.3 copy-start.6
  388.1 2.6 copy-start.9
  388.1 2.6 copy-start.10
  390.7 2.2 copy-start.17
  390.7 2.2 copy-start.18
  392.9 65.0 %copy-start.13 = (f32[4,1,1280]{2,1,0:T(1,128)S(1)}, f32[4,1,1280]{2,1,0:T(1,128)}, u32[]{:S(2)}) copy-start(f32[4,1,1280]{2,1,0:T(1,128)} %get-tuple-element.154) | copy-start | bytes 61444
  501.7 3.5 copy-start.12
  501.8 5.4 %copy-start.5 = (bf16[1,3,176,1024]{3,2,1,0:T(8,128)(2,1)S(1)}, bf16[1,3,176,1024]{3,2,1,0:T(8,128)(2,1)}, u32[]{:S(2)}) copy-start(bf16[1,3,176,1024]{3,2,1,0:T(8,128)(2,1)} %reduce-scatter.3.cloned.1.call-done) | copy-start | bytes 3244036
  509.7 2.6 copy-start.1
  509.7 1.8 copy-start.8
Sparse Core Ops, SparseCore 0:
  214.7 76.1 reduce-scatter.2
  293.2 96.2 reduce-scatter.4
where the time goes:
time: 528 us; the launch traced here: 519 us
  Pallas kernels  466 us (88%)
  local copies, waits for them, and re-layouts  22.9 us (4%)
  between operations  14.6 us (3%)
  other arithmetic  7.16 us (1%)
  waiting for transfers between devices  5.52 us (1%)
    pallas_call x1, Pallas kernels, front(): pl.pallas_call(functools.partial(front_kernel, scale, head_size, slots),...  115 us
    pallas_call x1, Pallas kernels, second_back(): pl.pallas_call(held(functools.partial(second_kernel, scale, head_size, sl...  65 us
    pallas_call x1, Pallas kernels, hidden_back(): pl.pallas_call(functools.partial(hidden_kernel, experts, scale, head_size...  64.7 us
    pallas_call x2, Pallas kernels, run_experts(): pl.pallas_call(functools.partial(expert_kernel, experts, units, len(kept)...  57.4 us
    pallas_call x1, Pallas kernels, return_rows(): pl.pallas_call(held(functools.partial(return_kernel, experts, slots), 1 +...  50.2 us
    pallas_call x1, Pallas kernels, final_back(): pl.pallas_call(functools.partial(final_kernel, slots), grid=(1,), in_spec...  41.6 us
    pallas_call x2, Pallas kernels, weight_grads(): pl.pallas_call(held(weight_kernel, 3, len(waits)), grid=(3,), in_specs=[p...  36.8 us
    pallas_call x1, Pallas kernels, own_experts(): pl.pallas_call(functools.partial(own_kernel, experts, units), grid=(1,),...  35.5 us
  transfers between devices with their start and end apart: 8, of which 1 were waited for; matrix products, arithmetic and copies ran while one was open for 3% of the time, Pallas kernels for 57%

commit v1 on v0

--- a/solution.py
+++ b/solution.py
@@ -915,7 +915,7 @@
     shares = back[:, model_width:]
     logit_grads = probs * (shares - jnp.sum(probs * shares, axis=1, keepdims=True))
     logit_grads = logit_grads.astype(jnp.bfloat16)
-    router_grad_ref[...] = dot_tn(normed, logit_grads)
+    router_grad_ref[...] = dot_tn(logit_grads, normed)
     grads = back[:, :model_width] + dot_nt(logit_grads, router_ref[...])
     hidden = hidden_ref[...]
     scale_rows = root_scale(hidden)
@@ -945,7 +945,8 @@
     refs = refs[3 * slots :]
     own_out, rest_out, refs = refs[:slots], refs[slots : 4 * slots], refs[4 * slots :]
     outs = [refs[4 * s : 4 * s + 4] for s in range(slots)]
-    mixed, refs = refs[4 * slots : 5 * slots], refs[5 * slots :]
+    mixed = [slot_of(refs[4 * slots], s, slots) for s in range(slots)]
+    refs = refs[4 * slots + 1 :]
     ring_ref, line_ref, rest_ref, leaving, arriving, attended, sems = refs[:7]
     got, far, last, low, out_sems = refs[7:12]
     qkv_ref, bias_ref, full_ref, total_ref, held_out, load_sems = refs[12:18]
@@ -1054,15 +1055,15 @@
         ]
         + [whole] * (len(each) - 4 * slots)
         + [pl.BlockSpec(memory_space=pl.ANY)] * (4 * slots),
-        out_specs=[whole] * (5 * slots + 3),
+        out_specs=[whole] * (4 * slots + 4),
         out_shape=[
             jax.ShapeDtypeStruct((span_rows, model_width), f32),
             jax.ShapeDtypeStruct((span_rows, model_width), bf16),
-            jax.ShapeDtypeStruct((model_width, router.shape[1]), f32),
+            jax.ShapeDtypeStruct((router.shape[1], model_width), f32),
             jax.ShapeDtypeStruct((1, model_width), f32),
         ]
         * slots
-        + [jax.ShapeDtypeStruct((span_rows, model_width), bf16)] * slots
+        + [jax.ShapeDtypeStruct((span_rows, slots * model_width), bf16)]
         + [
             jax.ShapeDtypeStruct(qkvs.shape[1:], bf16),
             jax.ShapeDtypeStruct((heads, 1, bias.shape[2] + span_rows), f32),
@@ -1087,7 +1088,7 @@
         compiler_params=remote_params(1),
         name="hidden_back",
     )(lengths, gain, router, w_attn, qkvs, bias, full, total, *each)
-    return [got[4 * s : 4 * s + 4] for s in range(slots)], got[4 * slots : 5 * slots], got[5 * slots :]
+    return [got[4 * s : 4 * s + 4] for s in range(slots)], got[4 * slots], got[4 * slots + 1 :]
 
 
 def near_others(dp, ep):
@@ -1104,10 +1105,12 @@
     *refs,
 ):
     attended, proj, refs = refs[:slots], refs[slots : 2 * slots], refs[2 * slots :]
-    ring_ref, line_ref, arrived_ref, early_ref, weight_ref, rows_ref = refs[:6]
+    own_w_all, gain_ref, refs = refs[0], refs[1], refs[2:]
+    ring_ref, line_ref, arrived_ref, early_ref, weight_ref, rows_ref, gain_grad_ref = refs[:7]
+    refs = refs[1:]
     sums, low, got_core, got_x, got_y, leaving, coming, sems, near_sems, last_sems = refs[6:16]
-    early_sems, held_refs, work = refs[16], refs[17:23], refs[23:]
-    normed_ref, qkv_ref, bias_ref, full_ref, total_ref, load_sems = held_refs
+    early_sems, held_refs, work = refs[16], refs[17:24], refs[24:]
+    normed_ref, qkv_ref, bias_ref, full_ref, total_ref, own_w_ref, load_sems = held_refs
     count = qkv_ref.shape[0]
     mine = lax.axis_index("cp")
     loads = [
@@ -1118,7 +1121,8 @@
                 (bias_all, bias_ref),
                 (full_all.at[1], full_ref),
                 (total_all.at[1], total_ref),
-                (normed_all.at[0], normed_ref),
+                (normed_all, normed_ref),
+                (own_w_all, own_w_ref),
             )
         )
     ]
@@ -1204,10 +1208,19 @@
     for copy in last:
         copy.start()
     total = None
-    for j in range(count):
-        term = dot_tn(normed_ref[j], former_ref[j])
-        total = term if total is None else total + term
+    for slot, grads in ((0, former_ref), (1, ring_ref)):
+        for j in range(count):
+            term = dot_tn(normed_ref[slot, j], grads[j])
+            total = term if total is None else total + term
     weight_ref[...] = total
+    first_gain = lax.dot_general(
+        jnp.ones((8, total.shape[1]), jnp.float32),
+        total * own_w_ref[...].astype(jnp.float32),
+        (((1,), (1,)), ((), ())),
+        precision=lax.Precision.HIGHEST,
+        preferred_element_type=jnp.float32,
+    )
+    gain_grad_ref[...] = first_gain / gain_ref[...]
     for copy in last:
         copy.wait()
     for j in range(1, count):
@@ -1217,7 +1230,7 @@
 
 
 def second_back(
-    lengths, former, normed_all, qkvs, bias, grads, full, total, attended, proj, scale, head_size, waits=()
+    lengths, former, normed_all, qkvs, bias, grads, full, total, attended, proj, own_w, gain, scale, head_size, waits=()
 ):
     slots, count, span_rows, own_width = qkvs.shape
     model_width = normed_all.shape[3]
@@ -1227,7 +1240,7 @@
     rows_shape = (model_width // 8, own_width // 3)
     return pl.pallas_call(
         held(
-            functools.partial(second_kernel, scale, head_size, slots), 8 + 2 * slots, len(waits)
+            functools.partial(second_kernel, scale, head_size, slots), 10 + 2 * slots, len(waits)
         ),
         grid=(1,),
         in_specs=[
@@ -1241,8 +1254,9 @@
             some,
         ]
         + [whole] * (2 * slots)
+        + [some, whole]
         + anywhere(waits),
-        out_specs=[whole] * 6,
+        out_specs=[whole] * 7,
         out_shape=[
             jax.ShapeDtypeStruct(qkvs.shape[1:], bf16),
             jax.ShapeDtypeStruct((bias.shape[0], 1, bias.shape[2] + span_rows), f32),
@@ -1250,6 +1264,7 @@
             jax.ShapeDtypeStruct((count, span_rows, 384), bf16),
             jax.ShapeDtypeStruct((model_width, own_width), f32),
             jax.ShapeDtypeStruct(rows_shape, f32),
+            jax.ShapeDtypeStruct((8, model_width), f32),
         ],
         scratch_shapes=[
             pltpu.VMEM((model_width, model_width), f32),
@@ -1263,18 +1278,19 @@
             pltpu.SemaphoreType.DMA((2, 3)),
             pltpu.SemaphoreType.DMA((2, count)),
             pltpu.SemaphoreType.DMA((2, count)),
-            pltpu.VMEM(normed_all.shape[1:], bf16),
+            pltpu.VMEM(normed_all.shape, bf16),
             pltpu.VMEM(qkvs.shape[1:], bf16),
             pltpu.VMEM(bias.shape, f32),
             pltpu.VMEM(full.shape[1:], f32),
             pltpu.VMEM(full.shape[1:], f32),
-            pltpu.SemaphoreType.DMA((5,)),
+            pltpu.VMEM(own_w.shape, bf16),
+            pltpu.SemaphoreType.DMA((6,)),
         ]
         + backward_work(count, span_rows, head_size),
         cost_estimate=cost(20e9, 20e6),
         compiler_params=remote_params(2),
         name="second_back",
-    )(lengths, former, normed_all, qkvs, bias, grads, full, total, *attended, *proj, *waits)
+    )(lengths, former, normed_all, qkvs, bias, grads, full, total, *attended, *proj, own_w, gain, *waits)
 
 
 def token_body(mine, input_ref, hidden_ref, gain_ref, weight_ref, part_refs, own_ref, out_ref):
@@ -1297,23 +1313,21 @@
 
 
 def final_kernel(
-    slots, ring_ref, early_ref, normed_all, former_all, own_w_all, arrived_ref, blocks_ref, small_ref, gain_ref,
-    weight_all, tokens_ref, *refs
+    slots, ring_ref, early_ref, former_all, arrived_ref, blocks_ref, small_ref, gain_ref, weight_all, tokens_ref, *refs
 ):
     inputs = [slot_of(tokens_ref, s, slots) for s in range(slots)]
-    hidden_all, refs = refs[:slots], refs[slots:]
-    outs, refs = refs[:slots], refs[slots:]
+    hidden_all, out_ref, refs = refs[:slots], refs[slots], refs[slots + 1 :]
+    outs = [slot_of(out_ref, s, slots) for s in range(slots)]
     small_out, attn_out = refs[:2]
     coming, here, sum_blocks, low_blocks, small_now, small_in, sems, near_sems, small_sems = refs[2:11]
-    got_core, got_x, got_y, normed_ref, former_ref, own_w_ref, weight_ref, hidden_refs, load_sems = refs[11:]
+    got_core, low_halves, got_halves, low_ends, got_ends, half_sems = refs[11:17]
+    former_ref, weight_ref, hidden_refs, load_sems = refs[17:]
     hiddens = [hidden_refs.at[s] for s in range(slots)]
     loads = [
         pltpu.make_async_copy(source, target, load_sems.at[at])
         for at, (source, target) in enumerate(
             (
-                (normed_all.at[1], normed_ref),
                 (former_all, former_ref),
-                (own_w_all, own_w_ref),
                 (weight_all.at[:, pl.ds(0, weight_ref.shape[1])], weight_ref),
                 *((hidden_all[s], hiddens[s]) for s in range(slots)),
             )
@@ -1332,21 +1346,9 @@
     for copy in copies:
         copy.start()
 
-    for load in loads[:3]:
-        load.wait()
+    small_now[0] = small_ref[...]
+    loads[0].wait()
     total = former_ref[...]
-    for j in range(count):
-        total = total + dot_tn(normed_ref[j], ring_ref[j])
-    ones = jnp.ones((8, total.shape[1]), jnp.float32)
-    first_gain = lax.dot_general(
-        ones,
-        total * own_w_ref[...].astype(jnp.float32),
-        (((1,), (1,)), ((), ())),
-        precision=lax.Precision.HIGHEST,
-        preferred_element_type=jnp.float32,
-    )
-    row = lax.broadcasted_iota(jnp.int32, small_ref.shape, 0)
-    small_now[0] = jnp.where(row == 6, first_gain / gain_ref[...], small_ref[...])
     groups = total.shape[1] // 384
     for group in range(groups):
         for which in range(3):
@@ -1375,14 +1377,28 @@
         return push(small_now.at[at], small_in.at[at], small_sems.at[0, at], small_sems.at[1, at], stages[at])
 
     small_push(0).start()
-    for load in loads[3:]:
+    for load in loads[1:]:
         load.wait()
     token_body(mine, inputs[0], hiddens[0], gain_ref, weight_ref, [arrived_ref], arrived_ref, outs[0])
     first.wait()
     here[...] = sum_blocks[core] + got_core[...].astype(jnp.float32)
-    low_blocks[0, 0] = here[1 - across].astype(jnp.bfloat16)
-    second = push(low_blocks.at[0, 0], got_x, near_sems.at[0, 1], near_sems.at[1, 1], x_other)
-    second.start()
+    middle = here.shape[2] // 2
+    upper, lower = slice(0, middle), slice(middle, 2 * middle)
+    for at in range(2):
+        low_halves[0, at] = here[1 - across, at, upper].astype(jnp.bfloat16)
+        low_halves[1, at] = here[at, 1 - ep, lower].astype(jnp.bfloat16)
+
+    def half_copy(at):
+        source, target, other = (
+            (low_halves.at[0], got_halves.at[0], x_other),
+            (low_halves.at[1], got_halves.at[1], y_other),
+            (low_ends.at[0], got_ends.at[0], y_other),
+            (low_ends.at[1], got_ends.at[1], x_other),
+        )[at]
+        return push(source, target, half_sems.at[0, at], half_sems.at[1, at], other)
+
+    half_copy(0).start()
+    half_copy(1).start()
     for at in range(len(stages)):
         small_push(at).wait()
         now = small_now[at] + small_in[at]
@@ -1392,19 +1408,26 @@
         else:
             small_out[...] = now
         if at == 1:
-            second.wait()
-            sum_blocks[0, 0] = here[across] + got_x[...].astype(jnp.float32)
-            low_blocks[0, 1, 0] = sum_blocks[0, 0, 1 - ep].astype(jnp.bfloat16)
-            third = push(low_blocks.at[0, 1, 0], got_y, near_sems.at[0, 2], near_sems.at[1, 2], y_other)
-            third.start()
+            half_copy(0).wait()
+            for k in range(2):
+                here[across, k, upper] = here[across, k, upper] + got_halves[0, k].astype(jnp.float32)
+            low_ends[0] = here[across, 1 - ep, upper].astype(jnp.bfloat16)
+            half_copy(2).start()
+            half_copy(1).wait()
+            for k in range(2):
+                here[k, ep, lower] = here[k, ep, lower] + got_halves[1, k].astype(jnp.float32)
+            low_ends[1] = here[1 - across, ep, lower].astype(jnp.bfloat16)
+            half_copy(3).start()
     for copy in copies:
         copy.wait()
     token_body(mine, inputs[1], hiddens[1], gain_ref, weight_ref, [early_ref, coming], ring_ref, outs[1])
-    third.wait()
-    attn_out[...] = sum_blocks[0, 0, ep] + got_y[...].astype(jnp.float32)
-
-
-def final_back(ring, early, normed_all, former, own_w, arrived, blocks, small, gain, w_attn, inputs, hiddens):
+    half_copy(2).wait()
+    attn_out[upper] = here[across, ep, upper] + got_ends[0].astype(jnp.float32)
+    half_copy(3).wait()
+    attn_out[lower] = here[across, ep, lower] + got_ends[1].astype(jnp.float32)
+
+
+def final_back(ring, early, former, arrived, blocks, small, gain, w_attn, inputs, hiddens):
     count, span_rows, own_width = ring.shape
     slots = len(hiddens)
     model_width = hiddens[0].shape[1]
@@ -1421,8 +1444,6 @@
             whole,
             whole,
             some,
-            some,
-            some,
             whole,
             whole,
             whole,
@@ -1431,8 +1452,8 @@
             whole,
         ]
         + [some] * slots,
-        out_specs=[whole] * (slots + 2),
-        out_shape=[jax.ShapeDtypeStruct((span_rows, model_width), bf16)] * slots
+        out_specs=[whole] * 3,
+        out_shape=[jax.ShapeDtypeStruct((span_rows, slots * model_width), bf16)]
         + [jax.ShapeDtypeStruct(small.shape, f32), jax.ShapeDtypeStruct(tile, f32)],
         scratch_shapes=[
             pltpu.VMEM((count, span_rows, own_width - early.shape[2]), bf16),
@@ -1445,19 +1466,20 @@
             pltpu.SemaphoreType.DMA((2, 3)),
             pltpu.SemaphoreType.DMA((2, stages)),
             pltpu.VMEM((2, groups) + tile, bf16),
-            pltpu.VMEM((groups,) + tile, bf16),
-            pltpu.VMEM(tile, bf16),
-            pltpu.VMEM(normed_all.shape[1:], bf16),
+            pltpu.VMEM((2, 2, model_width // 2, 128), bf16),
+            pltpu.VMEM((2, 2, model_width // 2, 128), bf16),
+            pltpu.VMEM((2, model_width // 2, 128), bf16),
+            pltpu.VMEM((2, model_width // 2, 128), bf16),
+            pltpu.SemaphoreType.DMA((2, 4)),
             pltpu.VMEM(former.shape, f32),
-            pltpu.VMEM(own_w.shape, bf16),
             pltpu.VMEM((model_width, 3 * model_width), bf16),
             pltpu.VMEM((slots, span_rows, model_width), f32),
-            pltpu.SemaphoreType.DMA((4 + slots,)),
+            pltpu.SemaphoreType.DMA((2 + slots,)),
         ],
         cost_estimate=cost(20e9, 20e6),
         compiler_params=remote_params(3),
         name="final_back",
-    )(ring, early, normed_all, former, own_w, arrived, blocks, small, gain, w_attn, inputs, *hiddens)
+    )(ring, early, former, arrived, blocks, small, gain, w_attn, inputs, *hiddens)
 
 
 gelu_inner = 0.7978845608028654
@@ -1491,13 +1513,23 @@
     out_own, out_rest, refs = refs[:slots], refs[slots : 4 * slots], refs[4 * slots :]
     here, got, far, last, low = refs[:5]
     outs, load_sems, sems = refs[5 : 5 + held_pairs], refs[5 + held_pairs], refs[6 + held_pairs]
+    arriving, core_sems = refs[7 + held_pairs :]
     dp, ep = lax.axis_index("dp"), lax.axis_index("ep")
-    _, x_other, y_other = near_others(dp, ep)
+    core_other, x_other, y_other = near_others(dp, ep)
     base = ep * (experts * back[0].shape[2])
     loads = [
         pltpu.make_async_copy(source, target, load_sems.at[i])
-        for i, (source, target) in enumerate(zip(far_outs, outs))
+        for i, (source, target) in enumerate(zip(far_outs[:-1], outs[:-1]))
     ]
+
+    def core_copy(at):
+        if at == 3:
+            source, target = far_outs[-1], outs[-1]
+        else:
+            source, target = back[-1].at[0, at], arriving.at[0, at]
+        return push(source, target, core_sems.at[0, at], core_sems.at[1, at], core_other)
+
+    given = [*back[:-1], arriving]
     for load in loads:
         load.start()
 
@@ -1510,6 +1542,8 @@
         ]
 
     def place(held_refs, source, targets):
+        if held_refs is given and source > 0:
+            core_copy(source - 1).wait()
         place_body(base, target_ref.at[source], rows_of(held_refs, source), targets)
 
     firsts = [
@@ -1522,18 +1556,21 @@
         push(low.at[0], last.at[0], sems.at[0, 4], sems.at[1, 4], y_other),
         push(low.at[1], last.at[1], sems.at[0, 5], sems.at[1, 5], x_other),
     ]
-    greet(x_other, y_other)
+    greet(core_other, x_other, y_other)
+    for at in (2, 0, 1, 3):
+        core_copy(at).start()
     halves = lambda source: [here.at[source, s] for s in range(slots)]
-    place(back, 3, halves(3))
+    place(given, 3, halves(3))
     firsts[2].start()
     firsts[3].start()
-    place(back, 1, halves(1))
+    place(given, 1, halves(1))
     firsts[0].start()
-    place(back, 2, halves(2))
+    place(given, 2, halves(2))
     firsts[1].start()
-    place(back, 0, halves(0))
+    place(given, 0, halves(0))
     for load in loads:
         load.wait()
+    core_copy(3).wait()
     for at, (former, source) in enumerate(((2, 2), (3, 1))):
         firsts[former].wait()
         low[at] = (here[source, at].astype(jnp.float32) + far[at].astype(jnp.float32)).astype(jnp.bfloat16)
@@ -1571,7 +1608,8 @@
         ],
         scratch_shapes=[pltpu.VMEM((4, slots, span_rows, wide), bf16), half, half, half, half]
         + [pltpu.VMEM(a.shape, bf16) for a in outs]
-        + [pltpu.SemaphoreType.DMA((len(outs),)), pltpu.SemaphoreType.DMA((2, 6))],
+        + [pltpu.SemaphoreType.DMA((len(outs),)), pltpu.SemaphoreType.DMA((2, 6))]
+        + [pltpu.VMEM(backs[-1].shape, bf16), pltpu.SemaphoreType.DMA((2, 4))],
         cost_estimate=cost(20e9, 20e6),
         compiler_params=remote_params(4),
         name="return_rows",
@@ -1978,8 +2016,11 @@
             (e, e + 1),
         )
         weight_part = weight_grads(window, kept, e, n_cp, units, backs[-1:] + outs[-1:])
-        backs += with_theirs(rest[0], rest[1])
-        outs += with_theirs(rest[2], rest[3])
+        if e + 1 < exp_dev:
+            backs += with_theirs(rest[0], rest[1])
+            outs += with_theirs(rest[2], rest[3])
+        else:
+            backs, outs = [*backs, *rest[:2]], [*outs, *rest[2:]]
         weight_sums.append(lax.psum_scatter(weight_part, "cp", scatter_dimension=0, tiled=False))
         kept = after(kept, weight_part)
     back_rows, out_own, out_rest = return_rows(target_columns, backs, outs, slots, [weight_part])
@@ -2003,8 +2044,8 @@
         head_size,
     )
     hidden_grads, proj_grads, router_parts, gain_parts = zip(*got)
-    router_grad = sum(router_parts)[:, :experts].T
-    ring_second, line_second, arrived, early, weight_first, out_grad = second_back(
+    router_grad = sum(router_parts)[:experts]
+    ring_second, line_second, arrived, early, weight_part, out_grad, gain_part = second_back(
         lengths,
         ringed,
         normed_all,
@@ -2015,6 +2056,8 @@
         total,
         attended,
         proj_grads,
+        w_own,
+        gain_first,
         scale,
         head_size,
         weight_sums[:1],
@@ -2024,14 +2067,12 @@
     table_grad = jnp.einsum("hg,hb->gb", head_hot, table_grad, precision=exact)
     table_row = jnp.pad(table_grad.reshape(1, -1), ((0, 0), (0, model_width - table_grad.size)))
     small = jnp.concatenate(
-        [router_grad, sum(gain_parts), table_row, jnp.zeros((2, model_width), f32)], axis=0
-    )
-    *tokens_grad, small_sum, attn_sum = final_back(
+        [router_grad, sum(gain_parts), table_row, gain_part[:2]], axis=0
+    )
+    tokens_grad, small_sum, attn_sum = final_back(
         ring_second,
         early,
-        normed_all,
-        weight_first,
-        w_own,
+        weight_part,
         arrived,
         out_grad,
         small,
@@ -2048,8 +2089,8 @@
         jnp.stack([part[which].T.astype(f32) for part in weight_sums]) for which in range(3)
     )
     return (
-        jnp.stack(mixed, axis=1),
-        jnp.stack(tokens_grad, axis=1),
+        mixed.reshape(tokens.shape),
+        tokens_grad.reshape(tokens.shape),
         attn_sum,
         table_sum,
         gain_first_sum,

time: 528 us -> 514 us (0.973)
  Pallas kernels: 466 us -> 460 us
  waiting for transfers between devices: 5.52 us -> 0.07 us
    pallas_call x1, Pallas kernels: 41.6 us -> 29.8 us  [final_back(): pl.pallas_call(functools.partial(final_kernel, slots), grid=(1,), in_spec...]
    ppermute x6 -> x4, waiting for transfers between devices: 5.45 us -> 0.01 us  [send(): return lax.ppermute(values, axis, pairs)]
    reshape x0 -> x2, local copies, waits for them, and re-layouts: none -> 5.32 us  [the longest x1 2.71 us: fast_device(): tokens_grad.reshape(tokens.shape)]
    unnamed x44 -> x36, local copies, waits for them, and re-layouts: 13.3 us -> 8.44 us
  transfers between devices with their start and end apart: 8 -> 6, of which waited for: 1 -> 0; matrix products, arithmetic and copies ran while one was open for 3% -> 3% of each run, Pallas kernels for 57% -> 58%
where the time goes in v1:
time: 514 us; the launch traced here: 505 us
  Pallas kernels  460 us (89%)
  local copies, waits for them, and re-layouts  21.5 us (4%)
  between operations  14.5 us (3%)
  other arithmetic  6.38 us (1%)
    pallas_call x1, Pallas kernels, front(): pl.pallas_call(functools.partial(front_kernel, scale, head_size, slots),...  115 us
    pallas_call x1, Pallas kernels, hidden_back(): pl.pallas_call(functools.partial(hidden_kernel, experts, scale, head_size...  67.2 us
    pallas_call x1, Pallas kernels, second_back(): pl.pallas_call(held(functools.partial(second_kernel, scale, head_size, sl...  65.5 us
    pallas_call x2, Pallas kernels, run_experts(): pl.pallas_call(functools.partial(expert_kernel, experts, units, len(kept)...  57.5 us
    pallas_call x1, Pallas kernels, return_rows(): pl.pallas_call(held(functools.partial(return_kernel, experts, slots), 1 +...  53.5 us
    pallas_call x2, Pallas kernels, weight_grads(): pl.pallas_call(held(weight_kernel, 3, len(waits)), grid=(3,), in_specs=[p...  36.8 us
    pallas_call x1, Pallas kernels, own_experts(): pl.pallas_call(functools.partial(own_kernel, experts, units), grid=(1,),...  35.5 us
    pallas_call x1, Pallas kernels, final_back(): pl.pallas_call(functools.partial(final_kernel, slots), grid=(1,), in_spec...  29.8 us
  transfers between devices with their start and end apart: 6, of which 0 were waited for; matrix products, arithmetic and copies ran while one was open for 3% of the time, Pallas kernels for 58%

profile of v1, /device:TPU:0, one launch (start us, length us, event | category | flops | bytes accessed | tf_op | source)
XLA Modules:
  0.0 505.5 jit_solution(16846825540621965428)
XLA Ops:
  7.2 0.0 copy-start
  7.2 0.0 reduce-scatter.3.cloned.1.call-start
  7.3 0.1 iota_add_fusion
  7.3 0.1 add.62
  7.4 0.8 rev.3
  8.3 0.2 fusion.10
  8.5 0.5 fusion.1
  8.9 0.6 broadcast_in_dim.22.line_ref
  9.6 2.5 copy.31
  12.1 0.0 copy-done.6
  12.1 1.2 copy.32
  13.3 0.2 copy.28
  13.5 0.0 copy-done.12
  13.5 0.0 copy-done.13
  13.6 0.6 fusion.8.target_ref
  14.2 0.8 concatenate.9.refs_4_.router_ref
  14.9 114.7 %front.1 = (bf16[2,4,256,1024]{3,2,1,0:T(8,128)(2,1)}, bf16[2,4,256,768]{3,2,1,0:T(8,128)(2,1)}, f32[4,256,1024]{2,1,0:T(8,128)}, f32[2,4,256,256]{3,2,1,0:T(8,1...) custom-call(s32[2]{0:T(128)} %refs_0_.1, ...), custom_call_target="tpu_custom_call" | custom-call | flops 3000000000 | bytes 1000000 | tf_op jit(solution)/shard_map/front/pallas_call | solution.py:852
  129.6 35.5 %own_experts.1 = (bf16[2,1,320,1152]{3,2,1,0:T(8,128)(2,1)}, bf16[2,1,320,1152]{3,2,1,0:T(8,128)(2,1)}, bf16[2,1,320,1024]{3,2,1,0:T(8,128)(2,1)}, bf16[2,1,320,...) custom-call(bf16[1,2,320,1024]{3,2,1,0:T(8,128)(2,1)} %get-tuple-ele, ...), custom_call_target="tpu_custom_call" | custom-call | flops 1000000000 | bytes 800000 | tf_op jit(solution)/shard_map/own_experts/pallas_call | solution.py:1770
  165.1 0.4 collective-permute-start
  165.6 0.1 collective-permute-start.2
  165.7 0.6 pad_add_fusion.window_ref.refs_0_
  166.3 28.3 %expert_rows.2 = (bf16[1,3,320,1152]{3,2,1,0:T(8,128)(2,1)}, bf16[1,3,320,1152]{3,2,1,0:T(8,128)(2,1)}, bf16[1,3,320,1024]{3,2,1,0:T(8,128)(2,1)}, bf16[1,3,320,...) custom-call(s32[1]{0:T(128)} %bitcast.6.first_ref, ...), custom_call_target="tpu_custom_call", output_to_operand_aliasing={{4}: (10, {}), {5}: (11, {})} | custom-call | flops 3000000000 | bytes 1200000 | tf_op jit(solution)/shard_map/expert_rows/pallas_call | solution.py:1823
  194.6 0.0 collective-permute-done.2.refs_4_.refs_8_
  194.6 0.0 copy-start.4
  194.7 0.0 collective-permute-done.refs_3_.refs_2_
  194.7 1.0 copy-done.4
  195.7 0.5 copy-done.3
  196.2 18.3 %weight_grads.2 = bf16[4,3,176,1024]{3,2,1,0:T(8,128)(2,1)} custom-call(s32[2]{0:T(128)} %pad_add_fusion.window_ref.refs_0_, bf16[2,2,4,640,1024]{4,3,2,1,0:T(8,128)(2,1)} %get-tuple-element.110.refs_1_.refs_8_, bf16[3,2,4,640,768]{4,3,2,1,0:T(8,128)(2,1)} %get-tuple-element.111.refs_2_.refs_9_, bf16[2,1,320,1152]{3,2,1,0:T(8,128)(2,1)} %copy-done.3, ...), custom_call_target="tpu_custom_call" | custom-call | flops 1000000000 | bytes 1000000 | tf_op jit(solution)/shard_map/weight_grads/pallas_call | solution.py:1869
  214.5 0.0 reduce-scatter.3.cloned.1.call-update
  214.5 0.0 reduce-scatter.5.cloned.1.call-start
  214.6 0.4 collective-permute-start.1
  215.0 0.1 collective-permute-start.3
  215.1 29.1 %expert_rows.3 = (bf16[1,3,320,1152]{3,2,1,0:T(8,128)(2,1)}, bf16[1,3,320,1152]{3,2,1,0:T(8,128)(2,1)}, bf16[1,3,320,1024]{3,2,1,0:T(8,128)(2,1)}, bf16[1,3,320,...) custom-call(s32[1]{0:T(128)S(6)} %add.64.first_ref, ...), custom_call_target="tpu_custom_call", output_to_operand_aliasing={{4}: (10, {}), {5}: (11, {})} | custom-call | flops 3000000000 | bytes 1200000 | tf_op jit(solution)/shard_map/expert_rows/pallas_call | solution.py:1823
  244.2 0.0 collective-permute-done.3.refs_4_.refs_10_
  244.3 0.0 collective-permute-done.1.refs_3_.refs_4_
  244.3 1.4 copy-done.2
  245.7 18.6 %weight_grads.3.refs_13_ = bf16[4,3,176,1024]{3,2,1,0:T(8,128)(2,1)} custom-call(s32[2]{0:T(128)} %pad_add_fusion.window_ref.refs_0_, bf16[2,2,4,640,1024]{4,3,2,1,0:T(8,128)(2,1)} %get-tuple-element.119.refs_1_, bf16[3,2,4,640,768]{4,3,2,1,0:T(8,128)(2,1)} %get-tuple-element.120.refs_2_, bf16[1,3,320,1152]{3,2,1,0:T(8,128)(2,1)} %copy-done.2, ...), custom_call_target="tpu_custom_call" | custom-call | flops 1000000000 | bytes 1000000 | tf_op jit(solution)/shard_map/weight_grads/pallas_call | solution.py:1869
  264.3 0.0 reduce-scatter.5.cloned.1.call-update
  264.3 0.7 copy-done.8
  265.0 1.3 copy.29
  266.3 53.5 %return_rows.1 = (f32[256,1152]{1,0:T(8,128)}, f32[256,1152]{1,0:T(8,128)}, bf16[256,1024]{1,0:T(8,128)(2,1)}, bf16[256,1024]{1,0:T(8,128)(2,1)}, bf16[256,1024]...) custom-call(s32[4,512,2]{2,1,0:T(8,128)} %bitcast.67, ...), custom_call_target="tpu_custom_call" | custom-call | flops 1000000000 | bytes 1000000 | tf_op jit(solution)/shard_map/return_rows/pallas_call | solution.py:1597
  319.8 67.2 %hidden_back.1 = (f32[256,1024]{1,0:T(8,128)}, bf16[256,1024]{1,0:T(8,128)(2,1)}, f32[128,1024]{1,0:T(8,128)}, f32[1,1024]{1,0:T(1,128)}, f32[256,1024]{1,0:T(8,...) custom-call(s32[2]{0:T(128)} %refs_0_.1, ...), custom_call_target="tpu_custom_call" | custom-call | flops 1000000000 | bytes 1000000 | tf_op jit(solution)/shard_map/hidden_back/pallas_call | solution.py:1046
  387.1 2.6 reshape.91
  389.7 0.0 copy-done.15
  389.7 0.8 slice_add_fusion.1
  390.5 65.5 %second_back.1 = (bf16[4,256,768]{2,1,0:T(8,128)(2,1)}, f32[4,1,1280]{2,1,0:T(1,128)}, bf16[4,256,768]{2,1,0:T(8,128)(2,1)}, bf16[4,256,384]{2,1,0:T(8,128)(2,1)...) custom-call(s32[2]{0:T(128)} %refs_0_.1, bf16[4,256,768]{2,1,0:T(8,128)(2,1)} %get-tuple-element.135.refs_1_, ...), custom_call_target="tpu_custom_call" | custom-call | flops 1000000000 | bytes 1000000 | tf_op jit(solution)/shard_map/second_back/pallas_call | solution.py:1241
  456.0 0.7 slice_add_fusion
  456.8 0.4 fusion
  457.1 0.3 fusion.9
  457.4 0.1 reshape.92
  457.5 0.8 slice.47
  458.3 0.6 fusion.4.small_ref
  458.9 29.8 %final_back.1 = (bf16[256,2048]{1,0:T(8,128)(2,1)}, f32[8,1024]{1,0:T(8,128)}, f32[1024,128]{1,0:T(8,128)}) custom-call(bf16[4,256,768]{2,1,0:T(8,128)(2,1)} %get-tuple-element.143.ring_ref, bf16[4,256,384]{2,1,0:T(8,128)(2,1)} %get-tuple-element.144.early_ref, f32[1024,768]{1,0:T(8,128)} %get-tuple-element.145.former_all, ...), custom_call_target="tpu_custom_call" | custom-call | flops 1000000000 | bytes 1000000 | tf_op jit(solution)/shard_map/final_back/pallas_call | solution.py:1440
  488.7 2.7 reshape.93
  491.4 0.0 copy-done.9
  491.4 0.7 reshape_squeeze.3
  492.1 0.6 fusion.13
  492.7 0.6 slice_bitcast_fusion.6
  493.3 0.1 slice_bitcast_fusion.1
  493.4 0.0 reduce-scatter.5.cloned.1.call-done
  493.4 1.3 slice_bitcast_fusion
  494.7 1.2 maximum_convert_fusion.2
  495.9 1.8 maximum_convert_fusion
  497.7 0.8 copy.42
  (26 shorter events, 0.1 us)
Async XLA Ops:
  7.2 1.1 copy-start
  7.2 4.9 copy-start.6
  7.2 383.3 %reduce-scatter.3.cloned.1.call-start = ((), (), s32[]{:S(2)}) async-start(), calls=%async_computation.2 | async-start | bytes 5406720 | tf_op jit(solution)/shard_map/reduce_scatter | solution.py:2024
  9.6 3.8 copy-start.11
  9.6 4.0 copy-start.12
  9.6 4.0 copy-start.13
  165.1 29.5 %collective-permute-start = (bf16[2,1,320,1152]{3,2,1,0:T(8,128)(2,1)}, bf16[2,1,320,1152]{3,2,1,0:T(8,128)(2,1)S(1)}, u32[]{:S(2)}, u32[]{:S(2)}) collective-permute-start(bf16[2,1,320,1152]{3,2,1,0:T(8,128)(2,1)} %get-tuple-element.98), channel_id=1, source_target_pairs={{0,8},{8,0},{16,24},{24,16},{1,9},{9,1},{17,25},{25,17},{2,10},{10... | collective-permute-start | bytes 4423688 | tf_op jit(solution)/shard_map/ppermute | solution.py:1888
  165.6 29.1 %collective-permute-start.2 = (bf16[2,1,320,1024]{3,2,1,0:T(8,128)(2,1)}, bf16[2,1,320,1024]{3,2,1,0:T(8,128)(2,1)S(1)}, u32[]{:S(2)}, u32[]{:S(2)}) collective-permute-start(bf16[2,1,320,1024]{3,2,1,0:T(8,128)(2,1)} %get-tuple-element.109), channel_id=1, source_target_pairs={{0,8},{8,0},{16,24},{24,16},{1,9},{9,1},{17,25},{25,17},{2,10},{10... | collective-permute-start | bytes 3932168 | tf_op jit(solution)/shard_map/ppermute | solution.py:1888
  194.6 1.1 copy-start.4
  194.7 1.5 copy-start.3
  214.5 278.9 %reduce-scatter.5.cloned.1.call-start = ((), (), s32[]{:S(2)}) async-start(), calls=%async_computation.3 | async-start | bytes 5406720 | tf_op jit(solution)/shard_map/reduce_scatter | solution.py:2024
  214.6 29.7 %collective-permute-start.1 = (bf16[1,3,320,1152]{3,2,1,0:T(8,128)(2,1)}, bf16[1,3,320,1152]{3,2,1,0:T(8,128)(2,1)S(1)}, u32[]{:S(2)}, u32[]{:S(2)}) collective-permute-start(bf16[1,3,320,1152]{3,2,1,0:T(8,128)(2,1)} %get-tuple-element.106), channel_id=1, source_target_pairs={{0,8},{8,0},{16,24},{24,16},{1,9},{9,1},{17,25},{25,17},{2,10},{10... | collective-permute-start | bytes 6635528 | tf_op jit(solution)/shard_map/ppermute | solution.py:1888
  215.0 29.3 %collective-permute-start.3 = (bf16[1,3,320,1024]{3,2,1,0:T(8,128)(2,1)}, bf16[1,3,320,1024]{3,2,1,0:T(8,128)(2,1)}, u32[]{:S(2)}, u32[]{:S(2)}) collective-permute-start(bf16[1,3,320,1024]{3,2,1,0:T(8,128)(2,1)} %get-tuple-element.116), channel_id=1, source_target_pairs={{0,8},{8,0},{16,24},{24,16},{1,9},{9,1},{17,25},{25,17},{2,10},{10... | collective-permute-start | bytes 5898248 | tf_op jit(solution)/shard_map/ppermute | solution.py:1888
  244.3 1.4 copy-start.2
  264.3 0.7 copy-start.8
  387.1 2.6 copy-start.14
  387.1 2.6 copy-start.15
  390.5 65.5 %copy-start.10 = (f32[4,1,1280]{2,1,0:T(1,128)S(1)}, f32[4,1,1280]{2,1,0:T(1,128)}, u32[]{:S(2)}) copy-start(f32[4,1,1280]{2,1,0:T(1,128)} %get-tuple-element.152) | copy-start | bytes 61444
  488.7 2.7 copy-start.9
  488.7 4.6 copy-start.5
  495.9 2.6 copy-start.1
  495.9 1.8 copy-start.7
Sparse Core Ops, SparseCore 0:
  214.6 76.1 reduce-scatter.2
  293.1 96.2 reduce-scatter.4

commit v2 on v1

--- a/solution.py
+++ b/solution.py
@@ -645,9 +645,9 @@
     grads = [slot_of(cotangent_ref, s, slots) for s in range(slots)]
     stores_to, own_w, targets_ref = refs[:5], refs[5], refs[6]
     over_ref, up_ref = refs[7:9]
-    picks = [refs[9 + 2 * i : 11 + 2 * i] for i in range(3)]
-    outs = [refs[15 + 3 * s : 18 + 3 * s] for s in range(slots)]
-    refs = refs[15 + 3 * slots :]
+    picks = [refs[9 + 2 * i : 11 + 2 * i] for i in range(2)]
+    outs = [refs[13 + 3 * s : 16 + 3 * s] for s in range(slots)]
+    refs = refs[13 + 3 * slots :]
     low, arrived, near_grads, ring_sems, own_sems, give_sems, plane_sems, target_sems = refs[:8]
     core_sems, normed_sems, store_sems, *made = refs[8:]
     all_ref, qkv_ref, bias_ref, full_ref, total_ref = made
@@ -727,16 +727,14 @@
 
     _, experts, capacity, _ = picks[0][0].shape
     base = ep * (experts * capacity)
-    at_of = ((0, 0), (1, 0), (1, 1), (1, 2), (2, 0))
+    at_of = ((0, 0), (1, 0), (1, 1), (1, 2))
 
     def pick(source):
         if source == 0:
             parts = grads
-        elif source == 4:
-            parts = [outs[s][2] for s in range(slots)]
         else:
             parts = [near_grads.at[source - 1, s] for s in range(slots)]
-        chosen = [targets_ref.at[source % 4, s] for s in range(slots)]
+        chosen = [targets_ref.at[source, s] for s in range(slots)]
         group, at = at_of[source]
         pick_body(base, capacity, experts, chosen, parts, picks[group][0].at[at])
         core_copy(source).start()
@@ -784,6 +782,13 @@
         def after_pair(pair):
             for copy in gives(slot, pair):
                 copy.start()
+            if slot > 0:
+
+                @pl.when(pair == 0)
+                def _():
+                    project(slot - 1)
+                    for at in range(2):
+                        normed_copy(at).start()
 
         forward_body(
             mine, length_ref[slot], scale, head_size, qkv_ref.at[slot], bias_ref, low.at[slot],
@@ -813,11 +818,7 @@
                 copy.wait_recv()
             pick(3)
     attend(slots - 1)
-    project(0)
-    for at in range(2):
-        normed_copy(at).start()
-    project(1)
-    pick(4)
+    project(slots - 1)
     for s in range(slots):
         for hop in range(count - 1):
             hop_copy(s, hop).wait_send()
@@ -825,7 +826,7 @@
         copy.wait_send()
     for at in range(2):
         normed_copy(at).wait()
-    for source in range(5):
+    for source in range(4):
         core_copy(source).wait()
     store(2, 0).wait()
     for s in range(slots):
@@ -863,7 +864,7 @@
             whole,
             whole,
         ],
-        out_specs=[pl.BlockSpec(memory_space=pl.ANY)] * 5 + [whole] * (10 + 3 * slots),
+        out_specs=[pl.BlockSpec(memory_space=pl.ANY)] * 5 + [whole] * (8 + 3 * slots),
         out_shape=[
             *(shape(*kind) for kind in made),
             shape((model_width, own_width), bf16),
@@ -872,7 +873,7 @@
         + [shape((span_rows, model_width), bf16)] * 2
         + [
             shape((sources, experts, capacity, model_width), bf16)
-            for sources in (1, 3, 1)
+            for sources in (1, 3)
             for _ in range(2)
         ]
         + [
@@ -890,8 +891,8 @@
             pltpu.SemaphoreType.DMA((2, slots, groups, count)),
             pltpu.SemaphoreType.DMA((2, 3, slots)),
             pltpu.SemaphoreType.DMA((2, 3, slots)),
-            pltpu.SemaphoreType.DMA((2, 5)),
-            pltpu.SemaphoreType.DMA((2, 3)),
+            pltpu.SemaphoreType.DMA((2, 4)),
+            pltpu.SemaphoreType.DMA((2, 2)),
             pltpu.SemaphoreType.DMA((5, slots)),
             *(pltpu.VMEM(*kind) for kind in made),
         ],
@@ -899,8 +900,8 @@
         compiler_params=remote_params(0),
         name="front",
     )(lengths, gain_first, gain_second, lines, target, w_attn, w_attn, inputs, grads)
-    pairs = [got[9 + 2 * i : 11 + 2 * i] for i in range(3)]
-    return got[:9], pairs, [got[15 + 3 * s : 18 + 3 * s] for s in range(slots)]
+    pairs = [got[9 + 2 * i : 11 + 2 * i] for i in range(2)]
+    return got[:9], pairs, [got[13 + 3 * s : 16 + 3 * s] for s in range(slots)]
 
 
 def hidden_body(
@@ -1666,11 +1667,12 @@
 
 
 def own_kernel(experts, own_units, *refs):
-    given, router_ref, weights, refs = refs[:4], refs[4], refs[5:8], refs[8:]
-    target_ref, over_ref, up_ref, normed_ref, refs = refs[0], refs[1], refs[2], refs[3], refs[4:]
+    given_grads, router_ref, weights, refs = refs[:2], refs[2], refs[3:6], refs[6:]
+    target_ref, over_ref, up_ref, first_ref, normed_ref, refs = *refs[:5], refs[5:]
     results, kept, (mine_ref, theirs_ref), refs = refs[:4], refs[4:6], refs[6:8], refs[8:]
     coming, picked, held_w, held_rows, held_units = refs[:5]
-    sems, core_sems, home_sems, load_sems, keep_sems = refs[5:]
+    sems, core_sems, home_sems, load_sems, keep_sems, own_picked, own_sems = refs[5:]
+    given = [own_picked.at[0], own_picked.at[1], *given_grads]
     exp_dev, capacity = picked.shape[1:3]
     dp, ep = lax.axis_index("dp"), lax.axis_index("ep")
     core_other, x_other, y_other = near_others(dp, ep)
@@ -1705,6 +1707,12 @@
     greet(core_other, x_other, y_other)
     for at in range(3):
         copy(at).start()
+    base = ep * (exp_dev * capacity)
+    chosen = [target_ref.at[0, s] for s in range(target_ref.shape[1])]
+    pick_body(base, capacity, exp_dev, chosen, (first_ref, normed_ref), own_picked.at[0, 0])
+    own_copy = push(own_picked.at[0], own_picked.at[1], own_sems.at[0], own_sems.at[1], core_other)
+    own_copy.start()
+    own_copy.wait()
     for expert in range(exp_dev):
         if expert == 1:
             copy(1).wait_recv()
@@ -1725,7 +1733,6 @@
         for kind in range(2):
             keep(expert, kind).start()
 
-    base = ep * (exp_dev * capacity)
     blocks = (
         (over_ref, coming.at[0]),
         (up_ref, coming.at[1]),
@@ -1755,8 +1762,8 @@
             keep(expert, kind).wait()
 
 
-def own_experts(given, router, weights, target, over, up, normed, total, experts, units):
-    _, exp_dev, capacity, model_width = given[0].shape
+def own_experts(grads, router, weights, target, over, up, first, normed, total, experts, units):
+    _, exp_dev, capacity, model_width = grads[0].shape
     span_rows = normed.shape[0]
     wide_units = aligned_units(units)
     tile = 2 * capacity
@@ -1770,7 +1777,7 @@
     got = pl.pallas_call(
         functools.partial(own_kernel, experts, units),
         grid=(1,),
-        in_specs=[whole] * 5 + [some] * 3 + [whole] * 4,
+        in_specs=[whole] * 3 + [some] * 3 + [whole] * 5,
         out_specs=[whole] * 4 + [some] * 4,
         out_shape=[shape((exp_dev, 1, capacity, wide), bf16)] * 2
         + [shape((exp_dev, 1, capacity, model_width), bf16)] * 2
@@ -1788,11 +1795,13 @@
             pltpu.SemaphoreType.DMA((3,)),
             pltpu.SemaphoreType.DMA((exp_dev, 3)),
             pltpu.SemaphoreType.DMA((exp_dev, 2)),
+            pltpu.VMEM((2, 1, exp_dev, capacity, model_width), bf16),
+            pltpu.SemaphoreType.DMA((2,)),
         ],
         cost_estimate=cost(20e9, 16e6),
         compiler_params=remote_params(5),
         name="own_experts",
-    )(*given, router, *weights, target, over, up, normed)
+    )(*grads, router, *weights, target, over, up, first, normed)
     return got[:4], got[4:6], got[6:]
 
 
@@ -1953,7 +1962,7 @@
     target = target.transpose(1, 2, 0).astype(jnp.int32)
     (
         (normed_all, qkvs, bias, full, total, w_own, target_all, over_first, up_first),
-        (grads_own, grads_rest_rows, picked_own),
+        (grads_own, grads_rest_rows),
         fronts,
     ) = front(
         lengths,
@@ -1984,12 +1993,13 @@
 
     first = (my_ep * exp_dev).astype(jnp.int32).reshape(1)
     own, kept, picked_rest = own_experts(
-        (*picked_own, *grads_own),
+        grads_own,
         router_wide,
         (w_gate, w_up, w_down),
         target_all,
         over_first,
         up_first,
+        normed_second[0],
         normed_second[1],
         sources,
         experts,

time: 514 us -> 512 us (level)
  no operation moved by 1% of the time
where the time goes in v2:
time: 512 us; the launch traced here: 503 us
  Pallas kernels  458 us (89%)
  local copies, waits for them, and re-layouts  21.5 us (4%)
  between operations  14.5 us (3%)
  other arithmetic  6.38 us (1%)
    pallas_call x1, Pallas kernels, front(): pl.pallas_call(functools.partial(front_kernel, scale, head_size, slots),...  113 us
    pallas_call x1, Pallas kernels, hidden_back(): pl.pallas_call(functools.partial(hidden_kernel, experts, scale, head_size...  67.5 us
    pallas_call x1, Pallas kernels, second_back(): pl.pallas_call(held(functools.partial(second_kernel, scale, head_size, sl...  65.5 us
    pallas_call x2, Pallas kernels, run_experts(): pl.pallas_call(functools.partial(expert_kernel, experts, units, len(kept)...  57.5 us
    pallas_call x1, Pallas kernels, return_rows(): pl.pallas_call(held(functools.partial(return_kernel, experts, slots), 1 +...  53.5 us
    pallas_call x2, Pallas kernels, weight_grads(): pl.pallas_call(held(weight_kernel, 3, len(waits)), grid=(3,), in_specs=[p...  36.8 us
    pallas_call x1, Pallas kernels, own_experts(): pl.pallas_call(functools.partial(own_kernel, experts, units), grid=(1,),...  34.6 us
    pallas_call x1, Pallas kernels, final_back(): pl.pallas_call(functools.partial(final_kernel, slots), grid=(1,), in_spec...  29.4 us
  transfers between devices with their start and end apart: 6, of which 0 were waited for; matrix products, arithmetic and copies ran while one was open for 3% of the time, Pallas kernels for 58%

profile of v2, /device:TPU:0, one launch (start us, length us, event | category | flops | bytes accessed | tf_op | source)
XLA Modules:
  0.0 502.6 jit_solution(17005179679381259678)
XLA Ops:
  7.2 0.0 copy-start
  7.2 0.0 copy-start.6
  7.2 0.0 reduce-scatter.3.cloned.1.call-start
  7.3 0.1 iota_add_fusion
  7.3 0.1 add.62
  7.4 0.8 rev.3
  8.3 0.0 copy-done
  8.3 0.2 fusion.10
  8.5 0.5 fusion.1
  8.9 0.6 broadcast_in_dim.22.line_ref
  9.6 2.5 copy.31
  12.1 0.0 copy-done.6
  12.1 1.2 copy.32
  13.3 0.2 copy.28
  13.6 0.6 fusion.8.target_ref
  14.2 0.8 concatenate.9.refs_2_.refs_4_.router_ref
  14.9 112.9 %front.1 = (bf16[2,4,256,1024]{3,2,1,0:T(8,128)(2,1)}, bf16[2,4,256,768]{3,2,1,0:T(8,128)(2,1)}, f32[4,256,1024]{2,1,0:T(8,128)}, f32[2,4,256,256]{3,2,1,0:T(8,1...) custom-call(s32[2]{0:T(128)} %refs_0_.1, ...), custom_call_target="tpu_custom_call" | custom-call | flops 3000000000 | bytes 1000000 | tf_op jit(solution)/shard_map/front/pallas_call | solution.py:853
  127.8 34.6 %own_experts.1 = (bf16[2,1,320,1152]{3,2,1,0:T(8,128)(2,1)}, bf16[2,1,320,1152]{3,2,1,0:T(8,128)(2,1)}, bf16[2,1,320,1024]{3,2,1,0:T(8,128)(2,1)}, bf16[2,1,320,...) custom-call(bf16[1,2,320,1024]{3,2,1,0:T(8,128)(2,1)} %get-tuple-ele, ...), custom_call_target="tpu_custom_call" | custom-call | flops 1000000000 | bytes 800000 | tf_op jit(solution)/shard_map/own_experts/pallas_call | solution.py:1777
  162.4 0.4 collective-permute-start
  162.9 0.1 collective-permute-start.2
  163.0 0.6 pad_add_fusion.window_ref.refs_0_
  163.6 28.4 %expert_rows.2 = (bf16[1,3,320,1152]{3,2,1,0:T(8,128)(2,1)}, bf16[1,3,320,1152]{3,2,1,0:T(8,128)(2,1)}, bf16[1,3,320,1024]{3,2,1,0:T(8,128)(2,1)}, bf16[1,3,320,...) custom-call(s32[1]{0:T(128)} %bitcast.6.first_ref, ...), custom_call_target="tpu_custom_call", output_to_operand_aliasing={{4}: (10, {}), {5}: (11, {})} | custom-call | flops 3000000000 | bytes 1200000 | tf_op jit(solution)/shard_map/expert_rows/pallas_call | solution.py:1832
  191.9 0.0 collective-permute-done.2.refs_4_.refs_8_
  192.0 0.0 copy-start.4
  192.0 0.0 collective-permute-done.refs_3_.refs_2_
  192.0 1.0 copy-done.4
  193.0 0.5 copy-done.3
  193.5 18.5 %weight_grads.2 = bf16[4,3,176,1024]{3,2,1,0:T(8,128)(2,1)} custom-call(s32[2]{0:T(128)} %pad_add_fusion.window_ref.refs_0_, bf16[2,2,4,640,1024]{4,3,2,1,0:T(8,128)(2,1)} %get-tuple-element.107.refs_1_.refs_8_, bf16[3,2,4,640,768]{4,3,2,1,0:T(8,128)(2,1)} %get-tuple-element.108.refs_2_.refs_9_, bf16[2,1,320,1152]{3,2,1,0:T(8,128)(2,1)} %copy-done.3, ...), custom_call_target="tpu_custom_call" | custom-call | flops 1000000000 | bytes 1000000 | tf_op jit(solution)/shard_map/weight_grads/pallas_call | solution.py:1878
  212.0 0.0 reduce-scatter.3.cloned.1.call-update
  212.0 0.0 reduce-scatter.5.cloned.1.call-start
  212.1 0.4 collective-permute-start.1
  212.5 0.1 collective-permute-start.3
  212.6 29.1 %expert_rows.3 = (bf16[1,3,320,1152]{3,2,1,0:T(8,128)(2,1)}, bf16[1,3,320,1152]{3,2,1,0:T(8,128)(2,1)}, bf16[1,3,320,1024]{3,2,1,0:T(8,128)(2,1)}, bf16[1,3,320,...) custom-call(s32[1]{0:T(128)S(6)} %add.64.first_ref, ...), custom_call_target="tpu_custom_call", output_to_operand_aliasing={{4}: (10, {}), {5}: (11, {})} | custom-call | flops 3000000000 | bytes 1200000 | tf_op jit(solution)/shard_map/expert_rows/pallas_call | solution.py:1832
  241.8 0.0 collective-permute-done.3.refs_4_.refs_10_
  241.8 0.0 collective-permute-done.1.refs_3_.refs_4_
  241.8 1.4 copy-done.2
  243.2 18.3 %weight_grads.3.refs_13_ = bf16[4,3,176,1024]{3,2,1,0:T(8,128)(2,1)} custom-call(s32[2]{0:T(128)} %pad_add_fusion.window_ref.refs_0_, bf16[2,2,4,640,1024]{4,3,2,1,0:T(8,128)(2,1)} %get-tuple-element.116.refs_1_, bf16[3,2,4,640,768]{4,3,2,1,0:T(8,128)(2,1)} %get-tuple-element.117.refs_2_, bf16[1,3,320,1152]{3,2,1,0:T(8,128)(2,1)} %copy-done.2, ...), custom_call_target="tpu_custom_call" | custom-call | flops 1000000000 | bytes 1000000 | tf_op jit(solution)/shard_map/weight_grads/pallas_call | solution.py:1878
  261.5 0.0 copy-start.8
  261.6 0.0 reduce-scatter.5.cloned.1.call-update
  261.6 0.7 copy-done.8
  262.3 1.3 copy.29
  263.6 53.5 %return_rows.1 = (f32[256,1152]{1,0:T(8,128)}, f32[256,1152]{1,0:T(8,128)}, bf16[256,1024]{1,0:T(8,128)(2,1)}, bf16[256,1024]{1,0:T(8,128)(2,1)}, bf16[256,1024]...) custom-call(s32[4,512,2]{2,1,0:T(8,128)} %bitcast.67, ...), custom_call_target="tpu_custom_call" | custom-call | flops 1000000000 | bytes 1000000 | tf_op jit(solution)/shard_map/return_rows/pallas_call | solution.py:1598
  317.1 67.5 %hidden_back.1 = (f32[256,1024]{1,0:T(8,128)}, bf16[256,1024]{1,0:T(8,128)(2,1)}, f32[128,1024]{1,0:T(8,128)}, f32[1,1024]{1,0:T(1,128)}, f32[256,1024]{1,0:T(8,...) custom-call(s32[2]{0:T(128)} %refs_0_.1, ...), custom_call_target="tpu_custom_call" | custom-call | flops 1000000000 | bytes 1000000 | tf_op jit(solution)/shard_map/hidden_back/pallas_call | solution.py:1047
  384.6 2.6 reshape.91
  387.2 0.0 copy-done.14
  387.2 0.8 slice_add_fusion.1
  388.0 65.5 %second_back.1 = (bf16[4,256,768]{2,1,0:T(8,128)(2,1)}, f32[4,1,1280]{2,1,0:T(1,128)}, bf16[4,256,768]{2,1,0:T(8,128)(2,1)}, bf16[4,256,384]{2,1,0:T(8,128)(2,1)...) custom-call(s32[2]{0:T(128)} %refs_0_.1, bf16[4,256,768]{2,1,0:T(8,128)(2,1)} %get-tuple-element.131.refs_1_, ...), custom_call_target="tpu_custom_call" | custom-call | flops 1000000000 | bytes 1000000 | tf_op jit(solution)/shard_map/second_back/pallas_call | solution.py:1242
  453.5 0.7 slice_add_fusion
  454.3 0.4 fusion
  454.6 0.3 fusion.9
  454.9 0.1 reshape.92
  455.0 0.8 slice.47
  455.8 0.6 fusion.4.small_ref
  456.4 29.4 %final_back.1 = (bf16[256,2048]{1,0:T(8,128)(2,1)}, f32[8,1024]{1,0:T(8,128)}, f32[1024,128]{1,0:T(8,128)}) custom-call(bf16[4,256,768]{2,1,0:T(8,128)(2,1)} %get-tuple-element.139.ring_ref, bf16[4,256,384]{2,1,0:T(8,128)(2,1)} %get-tuple-element.140.early_ref, f32[1024,768]{1,0:T(8,128)} %get-tuple-element.141.former_all, ...), custom_call_target="tpu_custom_call" | custom-call | flops 1000000000 | bytes 1000000 | tf_op jit(solution)/shard_map/final_back/pallas_call | solution.py:1441
  485.8 2.7 reshape.93
  488.5 0.7 reshape_squeeze.3
  489.2 0.6 fusion.13
  489.8 0.6 slice_bitcast_fusion.6
  490.4 0.1 slice_bitcast_fusion.1
  490.5 0.0 reduce-scatter.5.cloned.1.call-done
  490.5 1.3 slice_bitcast_fusion
  491.8 1.2 maximum_convert_fusion.2
  493.0 1.8 maximum_convert_fusion
  494.7 0.8 copy.42
  (26 shorter events, 0.1 us)
Async XLA Ops:
  7.2 1.1 copy-start
  7.2 4.9 copy-start.6
  7.2 380.8 %reduce-scatter.3.cloned.1.call-start = ((), (), s32[]{:S(2)}) async-start(), calls=%async_computation.2 | async-start | bytes 5406720 | tf_op jit(solution)/shard_map/reduce_scatter | solution.py:2034
  9.6 3.8 copy-start.11
  9.6 4.0 copy-start.12
  9.6 4.0 copy-start.13
  162.4 29.5 %collective-permute-start = (bf16[2,1,320,1152]{3,2,1,0:T(8,128)(2,1)}, bf16[2,1,320,1152]{3,2,1,0:T(8,128)(2,1)S(1)}, u32[]{:S(2)}, u32[]{:S(2)}) collective-permute-start(bf16[2,1,320,1152]{3,2,1,0:T(8,128)(2,1)} %get-tuple-element.95), channel_id=1, source_target_pairs={{0,8},{8,0},{16,24},{24,16},{1,9},{9,1},{17,25},{25,17},{2,10},{10... | collective-permute-start | bytes 4423688 | tf_op jit(solution)/shard_map/ppermute | solution.py:1897
  162.9 29.1 %collective-permute-start.2 = (bf16[2,1,320,1024]{3,2,1,0:T(8,128)(2,1)}, bf16[2,1,320,1024]{3,2,1,0:T(8,128)(2,1)S(1)}, u32[]{:S(2)}, u32[]{:S(2)}) collective-permute-start(bf16[2,1,320,1024]{3,2,1,0:T(8,128)(2,1)} %get-tuple-element.106), channel_id=1, source_target_pairs={{0,8},{8,0},{16,24},{24,16},{1,9},{9,1},{17,25},{25,17},{2,10},{10... | collective-permute-start | bytes 3932168 | tf_op jit(solution)/shard_map/ppermute | solution.py:1897
  192.0 1.1 copy-start.4
  192.0 1.5 copy-start.3
  212.0 278.5 %reduce-scatter.5.cloned.1.call-start = ((), (), s32[]{:S(2)}) async-start(), calls=%async_computation.3 | async-start | bytes 5406720 | tf_op jit(solution)/shard_map/reduce_scatter | solution.py:2034
  212.1 29.7 %collective-permute-start.1 = (bf16[1,3,320,1152]{3,2,1,0:T(8,128)(2,1)}, bf16[1,3,320,1152]{3,2,1,0:T(8,128)(2,1)S(1)}, u32[]{:S(2)}, u32[]{:S(2)}) collective-permute-start(bf16[1,3,320,1152]{3,2,1,0:T(8,128)(2,1)} %get-tuple-element.103), channel_id=1, source_target_pairs={{0,8},{8,0},{16,24},{24,16},{1,9},{9,1},{17,25},{25,17},{2,10},{10... | collective-permute-start | bytes 6635528 | tf_op jit(solution)/shard_map/ppermute | solution.py:1897
  212.5 29.3 %collective-permute-start.3 = (bf16[1,3,320,1024]{3,2,1,0:T(8,128)(2,1)}, bf16[1,3,320,1024]{3,2,1,0:T(8,128)(2,1)}, u32[]{:S(2)}, u32[]{:S(2)}) collective-permute-start(bf16[1,3,320,1024]{3,2,1,0:T(8,128)(2,1)} %get-tuple-element.113), channel_id=1, source_target_pairs={{0,8},{8,0},{16,24},{24,16},{1,9},{9,1},{17,25},{25,17},{2,10},{10... | collective-permute-start | bytes 5898248 | tf_op jit(solution)/shard_map/ppermute | solution.py:1897
  241.8 1.4 copy-start.2
  261.5 0.7 copy-start.8
  384.6 2.6 copy-start.14
  384.6 2.6 copy-start.15
  388.0 65.5 %copy-start.10 = (f32[4,1,1280]{2,1,0:T(1,128)S(1)}, f32[4,1,1280]{2,1,0:T(1,128)}, u32[]{:S(2)}) copy-start(f32[4,1,1280]{2,1,0:T(1,128)} %get-tuple-element.148) | copy-start | bytes 61444
  485.7 2.7 copy-start.9
  485.8 4.6 copy-start.5
  493.0 2.6 copy-start.1
  493.0 1.8 copy-start.7
Sparse Core Ops, SparseCore 0:
  212.1 76.1 reduce-scatter.2
  290.6 96.2 reduce-scatter.4

commit v3 on v2

--- a/solution.py
+++ b/solution.py
@@ -1864,10 +1864,18 @@
 def weight_kernel(window_ref, rows_ref, units_ref, weight_ref, total):
     pieces, _, piece, model_width = weight_ref.shape
     units = units_ref[0, 0].reshape(-1, units_ref.shape[-1])
-    total[...] = dot_tn(units, rows_ref[0, 0].reshape(-1, model_width))
-    skip = pl.multiple_of(window_ref[1], 64)
-    for at in range(pieces):
-        weight_ref[at, 0] = total[pl.ds(skip + at * piece, piece), :].astype(jnp.bfloat16)
+    part = dot_tn(units, rows_ref[0, 0].reshape(-1, model_width))
+
+    @pl.when(pl.program_id(1) == 0)
+    def _():
+        total[...] = part
+
+    @pl.when(pl.program_id(1) == 1)
+    def _():
+        total[...] = total[...] + part
+        skip = pl.multiple_of(window_ref[1], 64)
+        for at in range(pieces):
+            weight_ref[at, 0] = total[pl.ds(skip + at * piece, piece), :].astype(jnp.bfloat16)
 
 
 def weight_grads(window, kept, expert, pieces, units, waits=()):
@@ -1877,14 +1885,16 @@
     shape = (pieces, 3, units // pieces, model_width)
     return pl.pallas_call(
         held(weight_kernel, 3, len(waits)),
-        grid=(3,),
+        grid=(3, 2),
         in_specs=[
             pl.BlockSpec(memory_space=pltpu.SMEM),
-            pl.BlockSpec((1, 1, tiles, tile, model_width), lambda i: (i // 2, expert, 0, 0, 0)),
-            pl.BlockSpec((1, 1, tiles, tile, wide_units), lambda i: (i, expert, 0, 0, 0)),
+            pl.BlockSpec(
+                (1, 1, tiles // 2, tile, model_width), lambda i, k: (i // 2, expert, k, 0, 0)
+            ),
+            pl.BlockSpec((1, 1, tiles // 2, tile, wide_units), lambda i, k: (i, expert, k, 0, 0)),
         ]
         + anywhere(waits),
-        out_specs=pl.BlockSpec((pieces, 1) + shape[2:], lambda i: (0, i, 0, 0)),
+        out_specs=pl.BlockSpec((pieces, 1) + shape[2:], lambda i, k: (0, i, 0, 0)),
         out_shape=jax.ShapeDtypeStruct(shape, jnp.bfloat16),
         scratch_shapes=[pltpu.VMEM((wide_units, model_width), jnp.float32)],
         cost_estimate=cost(20e9, 20e6),

time: 512 us -> 515 us (level)
  no operation moved by 1% of the time
where the time goes in v3:
time: 515 us; the launch traced here: 505 us
  Pallas kernels  460 us (89%)
  local copies, waits for them, and re-layouts  21.5 us (4%)
  between operations  14.5 us (3%)
  other arithmetic  6.38 us (1%)
    pallas_call x1, Pallas kernels, front(): pl.pallas_call(functools.partial(front_kernel, scale, head_size, slots),...  113 us
    pallas_call x1, Pallas kernels, hidden_back(): pl.pallas_call(functools.partial(hidden_kernel, experts, scale, head_size...  66.2 us
    pallas_call x1, Pallas kernels, second_back(): pl.pallas_call(held(functools.partial(second_kernel, scale, head_size, sl...  65.5 us
    pallas_call x2, Pallas kernels, run_experts(): pl.pallas_call(functools.partial(expert_kernel, experts, units, len(kept)...  57.5 us
    pallas_call x1, Pallas kernels, return_rows(): pl.pallas_call(held(functools.partial(return_kernel, experts, slots), 1 +...  53.5 us
    pallas_call x2, Pallas kernels, weight_grads(): pl.pallas_call(held(weight_kernel, 3, len(waits)), grid=(3, 2), in_specs=...  40 us
    pallas_call x1, Pallas kernels, own_experts(): pl.pallas_call(functools.partial(own_kernel, experts, units), grid=(1,),...  34.6 us
    pallas_call x1, Pallas kernels, final_back(): pl.pallas_call(functools.partial(final_kernel, slots), grid=(1,), in_spec...  30.4 us
  transfers between devices with their start and end apart: 6, of which 0 were waited for; matrix products, arithmetic and copies ran while one was open for 3% of the time, Pallas kernels for 58%

profile of v3, /device:TPU:0, one launch (start us, length us, event | category | flops | bytes accessed | tf_op | source)
XLA Modules:
  0.0 505.5 jit_solution(3223567238019912312)
XLA Ops:
  7.2 0.0 copy-start
  7.2 0.0 reduce-scatter.3.cloned.1.call-start
  7.3 0.1 iota_add_fusion
  7.3 0.1 add.62
  7.4 0.8 rev.3
  8.3 0.2 fusion.10
  8.5 0.5 fusion.1
  8.9 0.6 broadcast_in_dim.22.line_ref
  9.6 2.5 copy.31
  12.1 1.2 copy.32
  13.3 0.2 copy.28
  13.6 0.6 fusion.8.target_ref
  14.2 0.8 concatenate.9.refs_2_.refs_4_.router_ref
  14.9 112.9 %front.1 = (bf16[2,4,256,1024]{3,2,1,0:T(8,128)(2,1)}, bf16[2,4,256,768]{3,2,1,0:T(8,128)(2,1)}, f32[4,256,1024]{2,1,0:T(8,128)}, f32[2,4,256,256]{3,2,1,0:T(8,1...) custom-call(s32[2]{0:T(128)} %refs_0_.1, ...), custom_call_target="tpu_custom_call" | custom-call | flops 3000000000 | bytes 1000000 | tf_op jit(solution)/shard_map/front/pallas_call | solution.py:853
  127.8 34.6 %own_experts.1 = (bf16[2,1,320,1152]{3,2,1,0:T(8,128)(2,1)}, bf16[2,1,320,1152]{3,2,1,0:T(8,128)(2,1)}, bf16[2,1,320,1024]{3,2,1,0:T(8,128)(2,1)}, bf16[2,1,320,...) custom-call(bf16[1,2,320,1024]{3,2,1,0:T(8,128)(2,1)} %get-tuple-ele, ...), custom_call_target="tpu_custom_call" | custom-call | flops 1000000000 | bytes 800000 | tf_op jit(solution)/shard_map/own_experts/pallas_call | solution.py:1777
  162.4 0.4 collective-permute-start
  162.9 0.1 collective-permute-start.2
  163.0 0.6 pad_add_fusion.window_ref.refs_0_
  163.6 28.4 %expert_rows.2 = (bf16[1,3,320,1152]{3,2,1,0:T(8,128)(2,1)}, bf16[1,3,320,1152]{3,2,1,0:T(8,128)(2,1)}, bf16[1,3,320,1024]{3,2,1,0:T(8,128)(2,1)}, bf16[1,3,320,...) custom-call(s32[1]{0:T(128)} %bitcast.6.first_ref, ...), custom_call_target="tpu_custom_call", output_to_operand_aliasing={{4}: (10, {}), {5}: (11, {})} | custom-call | flops 3000000000 | bytes 1200000 | tf_op jit(solution)/shard_map/expert_rows/pallas_call | solution.py:1832
  191.9 0.0 collective-permute-done.2.refs_4_.refs_8_
  192.0 0.0 copy-start.4
  192.0 0.0 collective-permute-done.refs_3_.refs_2_
  192.0 1.0 copy-done.4
  193.0 0.5 copy-done.3
  193.5 20.1 %weight_grads.2 = bf16[4,3,176,1024]{3,2,1,0:T(8,128)(2,1)} custom-call(s32[2]{0:T(128)} %pad_add_fusion.window_ref.refs_0_, bf16[2,2,4,640,1024]{4,3,2,1,0:T(8,128)(2,1)} %get-tuple-element.107.refs_1_.refs_8_, bf16[3,2,4,640,768]{4,3,2,1,0:T(8,128)(2,1)} %get-tuple-element.108.refs_2_.refs_9_, bf16[2,1,320,1152]{3,2,1,0:T(8,128)(2,1)} %copy-done.3, ...), custom_call_target="tpu_custom_call" | custom-call | flops 1000000000 | bytes 1000000 | tf_op jit(solution)/shard_map/weight_grads/pallas_call | solution.py:1886
  213.6 0.0 reduce-scatter.3.cloned.1.call-update
  213.6 0.0 reduce-scatter.5.cloned.1.call-start
  213.7 0.4 collective-permute-start.1
  214.1 0.1 collective-permute-start.3
  214.3 29.1 %expert_rows.3 = (bf16[1,3,320,1152]{3,2,1,0:T(8,128)(2,1)}, bf16[1,3,320,1152]{3,2,1,0:T(8,128)(2,1)}, bf16[1,3,320,1024]{3,2,1,0:T(8,128)(2,1)}, bf16[1,3,320,...) custom-call(s32[1]{0:T(128)S(6)} %add.64.first_ref, ...), custom_call_target="tpu_custom_call", output_to_operand_aliasing={{4}: (10, {}), {5}: (11, {})} | custom-call | flops 3000000000 | bytes 1200000 | tf_op jit(solution)/shard_map/expert_rows/pallas_call | solution.py:1832
  243.4 0.0 collective-permute-done.3.refs_4_.refs_10_
  243.4 0.0 collective-permute-done.1.refs_3_.refs_4_
  243.4 0.0 copy-start.2
  243.4 1.4 copy-done.2
  244.8 19.9 %weight_grads.3.refs_13_ = bf16[4,3,176,1024]{3,2,1,0:T(8,128)(2,1)} custom-call(s32[2]{0:T(128)} %pad_add_fusion.window_ref.refs_0_, bf16[2,2,4,640,1024]{4,3,2,1,0:T(8,128)(2,1)} %get-tuple-element.116.refs_1_, bf16[3,2,4,640,768]{4,3,2,1,0:T(8,128)(2,1)} %get-tuple-element.117.refs_2_, bf16[1,3,320,1152]{3,2,1,0:T(8,128)(2,1)} %copy-done.2, ...), custom_call_target="tpu_custom_call" | custom-call | flops 1000000000 | bytes 1000000 | tf_op jit(solution)/shard_map/weight_grads/pallas_call | solution.py:1886
  264.7 0.0 reduce-scatter.5.cloned.1.call-update
  264.8 0.7 copy-done.8
  265.5 1.3 copy.29
  266.8 53.5 %return_rows.1 = (f32[256,1152]{1,0:T(8,128)}, f32[256,1152]{1,0:T(8,128)}, bf16[256,1024]{1,0:T(8,128)(2,1)}, bf16[256,1024]{1,0:T(8,128)(2,1)}, bf16[256,1024]...) custom-call(s32[4,512,2]{2,1,0:T(8,128)} %bitcast.67, ...), custom_call_target="tpu_custom_call" | custom-call | flops 1000000000 | bytes 1000000 | tf_op jit(solution)/shard_map/return_rows/pallas_call | solution.py:1598
  320.3 66.2 %hidden_back.1 = (f32[256,1024]{1,0:T(8,128)}, bf16[256,1024]{1,0:T(8,128)(2,1)}, f32[128,1024]{1,0:T(8,128)}, f32[1,1024]{1,0:T(1,128)}, f32[256,1024]{1,0:T(8,...) custom-call(s32[2]{0:T(128)} %refs_0_.1, ...), custom_call_target="tpu_custom_call" | custom-call | flops 1000000000 | bytes 1000000 | tf_op jit(solution)/shard_map/hidden_back/pallas_call | solution.py:1047
  386.4 0.0 copy-start.14
  386.5 0.0 copy-start.15
  386.5 2.6 reshape.91
  389.1 0.0 copy-done.14
  389.1 0.8 slice_add_fusion.1
  389.9 65.5 %second_back.1 = (bf16[4,256,768]{2,1,0:T(8,128)(2,1)}, f32[4,1,1280]{2,1,0:T(1,128)}, bf16[4,256,768]{2,1,0:T(8,128)(2,1)}, bf16[4,256,384]{2,1,0:T(8,128)(2,1)...) custom-call(s32[2]{0:T(128)} %refs_0_.1, bf16[4,256,768]{2,1,0:T(8,128)(2,1)} %get-tuple-element.131.refs_1_, ...), custom_call_target="tpu_custom_call" | custom-call | flops 1000000000 | bytes 1000000 | tf_op jit(solution)/shard_map/second_back/pallas_call | solution.py:1242
  455.4 0.7 slice_add_fusion
  456.2 0.4 fusion
  456.5 0.3 fusion.9
  456.8 0.1 reshape.92
  456.9 0.8 slice.47
  457.7 0.6 fusion.4.small_ref
  458.3 30.4 %final_back.1 = (bf16[256,2048]{1,0:T(8,128)(2,1)}, f32[8,1024]{1,0:T(8,128)}, f32[1024,128]{1,0:T(8,128)}) custom-call(bf16[4,256,768]{2,1,0:T(8,128)(2,1)} %get-tuple-element.139.ring_ref, bf16[4,256,384]{2,1,0:T(8,128)(2,1)} %get-tuple-element.140.early_ref, f32[1024,768]{1,0:T(8,128)} %get-tuple-element.141.former_all, ...), custom_call_target="tpu_custom_call" | custom-call | flops 1000000000 | bytes 1000000 | tf_op jit(solution)/shard_map/final_back/pallas_call | solution.py:1441
  488.7 2.7 reshape.93
  491.4 0.0 copy-done.9
  491.4 0.7 reshape_squeeze.3
  492.1 0.6 fusion.13
  492.7 0.6 slice_bitcast_fusion.6
  493.3 0.1 slice_bitcast_fusion.1
  493.4 0.0 reduce-scatter.5.cloned.1.call-done
  493.4 1.3 slice_bitcast_fusion
  494.7 1.2 maximum_convert_fusion.2
  495.9 1.8 maximum_convert_fusion
  497.7 0.8 copy.42
  (26 shorter events, 0.1 us)
Async XLA Ops:
  7.2 1.1 copy-start
  7.2 4.9 copy-start.6
  7.2 382.7 %reduce-scatter.3.cloned.1.call-start = ((), (), s32[]{:S(2)}) async-start(), calls=%async_computation.2 | async-start | bytes 5406720 | tf_op jit(solution)/shard_map/reduce_scatter | solution.py:2044
  9.6 3.8 copy-start.11
  9.6 4.0 copy-start.12
  9.6 4.0 copy-start.13
  162.4 29.5 %collective-permute-start = (bf16[2,1,320,1152]{3,2,1,0:T(8,128)(2,1)}, bf16[2,1,320,1152]{3,2,1,0:T(8,128)(2,1)S(1)}, u32[]{:S(2)}, u32[]{:S(2)}) collective-permute-start(bf16[2,1,320,1152]{3,2,1,0:T(8,128)(2,1)} %get-tuple-element.95), channel_id=1, source_target_pairs={{0,8},{8,0},{16,24},{24,16},{1,9},{9,1},{17,25},{25,17},{2,10},{10... | collective-permute-start | bytes 4423688 | tf_op jit(solution)/shard_map/ppermute | solution.py:1907
  162.9 29.1 %collective-permute-start.2 = (bf16[2,1,320,1024]{3,2,1,0:T(8,128)(2,1)}, bf16[2,1,320,1024]{3,2,1,0:T(8,128)(2,1)S(1)}, u32[]{:S(2)}, u32[]{:S(2)}) collective-permute-start(bf16[2,1,320,1024]{3,2,1,0:T(8,128)(2,1)} %get-tuple-element.106), channel_id=1, source_target_pairs={{0,8},{8,0},{16,24},{24,16},{1,9},{9,1},{17,25},{25,17},{2,10},{10... | collective-permute-start | bytes 3932168 | tf_op jit(solution)/shard_map/ppermute | solution.py:1907
  192.0 1.1 copy-start.4
  192.0 1.5 copy-start.3
  213.6 279.8 %reduce-scatter.5.cloned.1.call-start = ((), (), s32[]{:S(2)}) async-start(), calls=%async_computation.3 | async-start | bytes 5406720 | tf_op jit(solution)/shard_map/reduce_scatter | solution.py:2044
  213.7 29.7 %collective-permute-start.1 = (bf16[1,3,320,1152]{3,2,1,0:T(8,128)(2,1)}, bf16[1,3,320,1152]{3,2,1,0:T(8,128)(2,1)S(1)}, u32[]{:S(2)}, u32[]{:S(2)}) collective-permute-start(bf16[1,3,320,1152]{3,2,1,0:T(8,128)(2,1)} %get-tuple-element.103), channel_id=1, source_target_pairs={{0,8},{8,0},{16,24},{24,16},{1,9},{9,1},{17,25},{25,17},{2,10},{10... | collective-permute-start | bytes 6635528 | tf_op jit(solution)/shard_map/ppermute | solution.py:1907
  214.1 29.3 %collective-permute-start.3 = (bf16[1,3,320,1024]{3,2,1,0:T(8,128)(2,1)}, bf16[1,3,320,1024]{3,2,1,0:T(8,128)(2,1)}, u32[]{:S(2)}, u32[]{:S(2)}) collective-permute-start(bf16[1,3,320,1024]{3,2,1,0:T(8,128)(2,1)} %get-tuple-element.113), channel_id=1, source_target_pairs={{0,8},{8,0},{16,24},{24,16},{1,9},{9,1},{17,25},{25,17},{2,10},{10... | collective-permute-start | bytes 5898248 | tf_op jit(solution)/shard_map/ppermute | solution.py:1907
  243.4 1.4 copy-start.2
  264.7 0.7 copy-start.8
  386.4 2.6 copy-start.14
  386.5 2.6 copy-start.15
  389.9 65.5 %copy-start.10 = (f32[4,1,1280]{2,1,0:T(1,128)S(1)}, f32[4,1,1280]{2,1,0:T(1,128)}, u32[]{:S(2)}) copy-start(f32[4,1,1280]{2,1,0:T(1,128)} %get-tuple-element.148) | copy-start | bytes 61444
  488.7 2.7 copy-start.9
  488.7 4.6 copy-start.5
  495.9 2.6 copy-start.1
  495.9 1.8 copy-start.7
Sparse Core Ops, SparseCore 0:
  213.8 76.1 reduce-scatter.2
  292.3 96.2 reduce-scatter.4
